TPU v7x, 128 devices: a whole 4x4x4 slice. The times are simulated.
128 devices in a mesh: segment: 2 (over x_lo), dp: 16 (over z, y), vocab: 4 (over x_hi, core).
Axes of the slice: x: 4 (x_hi: 2, x_lo: 2; x = x_hi * 2 + x_lo), y: 4, z: 4, core: 2. Of those that a mesh axis runs over, the one named last changes fastest.
Arguments:
- patches: bfloat16 [2, 16, 36, 1152], P(None, 'dp'), may hold values from -6 to 6
- text_embed: bfloat16 [2, 16, 96, 4096], P(None, 'dp'), may hold values from -6 to 6
- mask_embed: bfloat16 [4096], replicated, may hold values from -6 to 6
- image_counts: int32 [2, 16], P(None, 'dp'), may hold values from 1 to 6
- image_order: int32 [2, 16, 6], P(None, 'dp'), may hold values from 0 to 5, each once within a row
- masked_positions: int32 [2, 16, 4], P(None, 'dp'), may hold values from 36 to 95, as said below
- ratio_index: int32 [2, 16], replicated, may hold values from 1 to 8
- enc_up: bfloat16 [2, 1152, 4304], P(None, None, 'vocab'), may hold values from -0.1875 to 0.1875
- enc_down: bfloat16 [2, 4304, 1152], P(None, 'vocab'), may hold values from -0.09375 to 0.09375
- projector: bfloat16 [1152, 4096], P(None, 'vocab'), may hold values from -0.1875 to 0.1875
- lang_qkv: bfloat16 [2, 3, 4096, 2048], P('segment', None, 'dp', 'vocab'), may hold values from -0.09375 to 0.09375
- lang_out: bfloat16 [2, 2048, 4096], P('segment', 'vocab', 'dp'), may hold values from -0.125 to 0.125
- head_weight: bfloat16 [32768, 4096], P(('segment', 'dp', 'vocab')), may hold values from -0.25 to 0.25
- teacher_logits: bfloat16 [128, 32768], P(None, ('segment', 'dp', 'vocab')), may hold values from -18 to 320
Outputs:
- loss: float32 [], replicated
- projector_grad: float32 [1152, 4096], P(('segment', 'dp'), 'vocab')
Inputs may be any that keep to these rules, and one draw needn't show every extreme that they name: `masked_positions`: distinct cells of the text part, from 36 on.
All inputs are finite; a program needn't handle non-finite values.
Results may differ from a plain program's by a relative error of at most 0.039.
Values may be sent and summed in bfloat16 or wider, within the bound.
No kernel may reach another device: no remote copies, remote signals or barrier semaphores. Data moves between devices by JAX's collectives and lax.ppermute only.
A program may use at most 128 MiB of HBM per device.

v0:
```python
import jax
import jax.numpy as jnp
from jax import lax
from jax.sharding import PartitionSpec as P

HD = 128
MASKED = 4
RATIOS = 8


epsilon = 1e-06
rope_base = 500000.0


def from_behind(block, axis, distance):
    devices = range(lax.axis_size(axis))
    route = [(i - distance, i) for i in devices if i - distance in devices]
    return lax.ppermute(block, axis, route)


def broadcast(block, axis, source):
    block = jnp.where(lax.axis_index(axis) == source, block, jnp.zeros_like(block))
    return lax.psum(block, axis)


def merged(part, axis, combine):
    gathered = jax.tree.map(lambda a: lax.all_gather(a, axis), part)

    def take(source):
        return jax.tree.map(lambda a: lax.dynamic_index_in_dim(a, source, 0, False), gathered)

    return lax.fori_loop(
        1, lax.axis_size(axis), lambda source, state: combine(state, take(source)), take(0)
    )


def norm_rows(values_in):
    return values_in * lax.rsqrt(jnp.mean(values_in * values_in, axis=-1, keepdims=True) + epsilon)


def layer_norm(values_in):
    centred = values_in - jnp.mean(values_in, axis=-1, keepdims=True)
    return centred * lax.rsqrt(jnp.mean(centred * centred, axis=-1, keepdims=True) + epsilon)


def norm_back(values_in, cotangent):
    factor = lax.rsqrt(jnp.mean(values_in * values_in, axis=-1, keepdims=True) + epsilon)
    return factor * cotangent - values_in * factor**3 * jnp.mean(
        cotangent * values_in, axis=-1, keepdims=True
    )


def rope_tables(length, head_size):
    halfway = head_size // 2
    inverse = rope_base ** (-2.0 * jnp.arange(halfway, dtype=jnp.float32) / head_size)
    angles = jnp.arange(length, dtype=jnp.float32)[:, None] * inverse[None, :]
    return (jnp.cos(angles)[:, None, :], jnp.sin(angles)[:, None, :])


def rotate(values_in, cosine, sine):
    halfway = values_in.shape[-1] // 2
    first_half = values_in[..., :halfway]
    second_half = values_in[..., halfway:]
    return jnp.concatenate(
        [first_half * cosine - second_half * sine, second_half * cosine + first_half * sine],
        axis=-1,
    )


def rotate_back(cotangent, cosine, sine):
    halfway = cotangent.shape[-1] // 2
    first_half = cotangent[..., :halfway]
    second_half = cotangent[..., halfway:]
    return jnp.concatenate(
        [first_half * cosine + second_half * sine, second_half * cosine - first_half * sine],
        axis=-1,
    )


def attend(queries, key_rows, value_rows):
    scores = jnp.einsum(
        "qhd,khd->hqk", queries.astype(jnp.float32), key_rows.astype(jnp.float32)
    ) * queries.shape[-1] ** (-0.5)
    probs = jax.nn.softmax(scores, axis=-1).astype(jnp.bfloat16)
    mixed = jnp.einsum("hqk,khd->qhd", probs.astype(jnp.float32), value_rows.astype(jnp.float32))
    return mixed.astype(jnp.bfloat16)


def attention_parts(hidden, qkv_weight, cosine, sine):
    seq_len = hidden.shape[0]
    heads_here = qkv_weight.shape[2] // HD
    shaped = (seq_len, heads_here, HD)
    normed = norm_rows(hidden.astype(jnp.float32)).astype(jnp.bfloat16)
    queries = rotate(
        jnp.dot(normed, qkv_weight[0], preferred_element_type=jnp.float32).reshape(shaped),
        cosine,
        sine,
    ).astype(jnp.bfloat16)
    key_rows = rotate(
        jnp.dot(normed, qkv_weight[1], preferred_element_type=jnp.float32).reshape(shaped),
        cosine,
        sine,
    ).astype(jnp.bfloat16)
    value_rows = (
        jnp.dot(normed, qkv_weight[2], preferred_element_type=jnp.float32)
        .astype(jnp.bfloat16)
        .reshape(shaped)
    )
    mixed = attend(queries, key_rows, value_rows).reshape(seq_len, heads_here * HD)
    return (queries, key_rows, value_rows, mixed)


def attention_back(gradient, queries, key_rows, value_rows, qkv_weight, out_weight, cosine, sine):
    seq_len = gradient.shape[0]
    d_mixed = jnp.dot(gradient, out_weight.T, preferred_element_type=jnp.float32).astype(
        jnp.bfloat16
    )
    pullback = jax.vjp(attend, queries, key_rows, value_rows)[1]
    d_query, d_key, d_value = pullback(d_mixed.reshape(queries.shape))
    d_query = (
        rotate_back(d_query.astype(jnp.float32), cosine, sine)
        .astype(jnp.bfloat16)
        .reshape(seq_len, -1)
    )
    d_key = (
        rotate_back(d_key.astype(jnp.float32), cosine, sine)
        .astype(jnp.bfloat16)
        .reshape(seq_len, -1)
    )
    d_value = d_value.reshape(seq_len, -1)
    partial_sum = jnp.dot(d_query, qkv_weight[0].T, preferred_element_type=jnp.float32)
    partial_sum = partial_sum + jnp.dot(d_key, qkv_weight[1].T, preferred_element_type=jnp.float32)
    return partial_sum + jnp.dot(d_value, qkv_weight[2].T, preferred_element_type=jnp.float32)


def build_sequence(image_rows, text_rows, mask_row, image_total, ordering, positions):
    seq_len = text_rows.shape[0]
    per_image = image_rows.shape[0] // ordering.shape[0]
    slot_ids = jnp.arange(image_rows.shape[0], dtype=jnp.int32)
    image_of = slot_ids // per_image
    target = jnp.take(ordering, image_of) * per_image + slot_ids % per_image
    is_live = image_of < image_total
    cell_ids = jnp.arange(seq_len, dtype=jnp.int32)
    matches = (target[None, :] == cell_ids[:, None]) & is_live[None, :]
    placing = matches.astype(jnp.bfloat16)
    filled = jnp.any(matches, axis=1)
    placed = jnp.dot(placing, image_rows, preferred_element_type=jnp.float32).astype(jnp.bfloat16)
    sequence = jnp.where(filled[:, None], placed, text_rows)
    masked = jnp.any(positions[None, :] == cell_ids[:, None], axis=1)
    sequence = jnp.where(masked[:, None], mask_row[None, :], sequence)
    return (sequence, placing)


def pick_matrix(positions, seq_len):
    return (positions[:, None] == jnp.arange(seq_len, dtype=jnp.int32)[None, :]).astype(
        jnp.bfloat16
    )


def encode_rows(patch_block, enc_up, enc_down):
    shape_in = patch_block.shape
    current = patch_block.reshape(-1, shape_in[-1])
    for layer in range(enc_up.shape[0]):
        normed = layer_norm(current.astype(jnp.float32)).astype(jnp.bfloat16)
        inner = jax.nn.gelu(
            jnp.dot(normed, enc_up[layer], preferred_element_type=jnp.float32), approximate=True
        ).astype(jnp.bfloat16)
        summed = lax.psum(
            jnp.dot(inner, enc_down[layer], preferred_element_type=jnp.float32).astype(
                jnp.bfloat16
            ),
            "vocab",
        ).astype(jnp.float32)
        current = (current.astype(jnp.float32) + summed).astype(jnp.bfloat16)
    return current.reshape(shape_in)


def join_parts(earlier, later):
    sum_student = earlier[0] + later[0]
    top_teacher = jnp.maximum(earlier[1], later[1])
    factor_early = jnp.exp(earlier[1] - top_teacher)
    factor_late = jnp.exp(later[1] - top_teacher)
    sum_teacher = earlier[2] * factor_early + later[2] * factor_late
    cross = earlier[3] * factor_early + later[3] * factor_late
    return (sum_student, top_teacher, sum_teacher, cross)


def shards(
    patches,
    text_embed,
    mask_embed,
    image_counts,
    image_order,
    masked_positions,
    ratio_index,
    enc_up,
    enc_down,
    projector,
    lang_qkv,
    lang_out,
    head_weight,
    teacher_logits,
):
    phase_count = lax.axis_size("segment")
    phase_index = lax.axis_index("segment")
    vocab_index = lax.axis_index("vocab")
    micro_count = text_embed.shape[0]
    seq_len = text_embed.shape[2]
    model_width = text_embed.shape[3]
    column_count = projector.shape[1]
    qkv_full, out_full = (
        lax.all_gather(lang_qkv, "dp", axis=2, tiled=True),
        lax.all_gather(lang_out, "dp", axis=2, tiled=True),
    )
    qkv_full = qkv_full[0]
    out_full = out_full[0]
    cosine, sine = rope_tables(seq_len, HD)
    encoded = encode_rows(patches, enc_up, enc_down)
    flat_rows = encoded.reshape(-1, encoded.shape[3])
    image_cols = (
        jnp.dot(flat_rows, projector, preferred_element_type=jnp.float32)
        .astype(jnp.bfloat16)
        .reshape(micro_count, -1, column_count)
    )
    images = lax.all_gather(image_cols, "vocab", axis=2, tiled=True)
    first_inputs = []
    placings = []
    pickers = []
    for micro_index in range(micro_count):
        sequence, placing = build_sequence(
            images[micro_index],
            text_embed[micro_index, 0],
            mask_embed,
            image_counts[micro_index, 0],
            image_order[micro_index, 0],
            masked_positions[micro_index, 0],
        )
        first_inputs.append(sequence)
        placings.append(placing)
        pickers.append(pick_matrix(masked_positions[micro_index, 0], seq_len))
    step_count = micro_count + phase_count - 1
    received = jnp.zeros((seq_len, model_width), jnp.bfloat16)
    saved_hidden, saved_queries, saved_keys, saved_values, finished = ([], [], [], [], [])
    for step in range(step_count):
        hidden = jnp.where(phase_index == 0, first_inputs[min(step, micro_count - 1)], received)
        queries, key_rows, value_rows, mixed = attention_parts(hidden, qkv_full, cosine, sine)
        partial_out = jnp.dot(mixed, out_full, preferred_element_type=jnp.float32)
        saved_hidden.append(hidden)
        saved_queries.append(queries)
        saved_keys.append(key_rows)
        saved_values.append(value_rows)
        branch = lax.psum(partial_out.astype(jnp.bfloat16), "vocab").astype(jnp.float32)
        output = (hidden.astype(jnp.float32) + branch).astype(jnp.bfloat16)
        finished.append(output)
        received = from_behind(output, "segment", 1)
    final_root = phase_count - 1
    last_rows = jnp.stack(
        [
            jnp.dot(
                pickers[micro_index],
                finished[micro_index + phase_count - 1],
                preferred_element_type=jnp.float32,
            )
            for micro_index in range(micro_count)
        ]
    ).astype(jnp.bfloat16)
    own_rows = broadcast(last_rows, "segment", final_root)
    all_rows = lax.all_gather(own_rows[:, None], "dp", axis=1, tiled=True)
    sample_count = all_rows.shape[1]
    row_data = all_rows.reshape(-1, model_width).astype(jnp.float32)
    final = norm_rows(row_data).astype(jnp.bfloat16)
    logits = jnp.dot(final, head_weight.T, preferred_element_type=jnp.float32)
    teacher = teacher_logits.astype(jnp.float32)
    sum_student = jnp.sum(jnp.exp(logits), axis=1)
    top_teacher = jnp.max(teacher, axis=1)
    teacher_weights = jnp.exp(teacher - top_teacher[:, None])
    sum_teacher = jnp.sum(teacher_weights, axis=1)
    cross = jnp.sum(teacher_weights * (teacher - logits), axis=1)
    sum_student, top_teacher, sum_teacher, cross = merged(
        (sum_student, top_teacher, sum_teacher, cross), ("segment", "dp", "vocab"), join_parts
    )
    norm_student = jnp.log(sum_student)
    norm_teacher = top_teacher + jnp.log(sum_teacher)
    divergence = cross / sum_teacher - norm_teacher + norm_student
    weights = jnp.repeat((RATIOS / ratio_index.astype(jnp.float32)).reshape(-1), MASKED)
    sequences = micro_count * sample_count
    loss = jnp.sum(weights * divergence) / sequences
    d_logits = (
        (weights / sequences)[:, None]
        * (jnp.exp(logits - norm_student[:, None]) - jnp.exp(teacher - norm_teacher[:, None]))
    ).astype(jnp.bfloat16)
    d_final = jnp.dot(d_logits, head_weight, preferred_element_type=jnp.float32).reshape(
        micro_count, sample_count, MASKED, model_width
    )
    d_own = lax.psum_scatter(
        d_final.astype(jnp.bfloat16), "dp", scatter_dimension=1, tiled=True
    ).astype(jnp.float32)
    d_own = lax.psum(d_own.astype(jnp.bfloat16), ("segment", "vocab")).astype(jnp.float32)[:, 0]
    d_rows = norm_back(own_rows.astype(jnp.float32), d_own)
    last_grads = [
        jnp.dot(
            pickers[micro_index].astype(jnp.float32).T,
            d_rows[micro_index],
            precision=lax.Precision.HIGHEST,
            preferred_element_type=jnp.float32,
        ).astype(jnp.bfloat16)
        for micro_index in range(micro_count)
    ]
    stack_hidden = jnp.stack(saved_hidden)
    stack_queries = jnp.stack(saved_queries)
    stack_keys = jnp.stack(saved_keys)
    stack_values = jnp.stack(saved_values)
    received = jnp.zeros((seq_len, model_width), jnp.bfloat16)
    results = []
    for step in range(step_count):
        gradient = jnp.where(
            phase_index == phase_count - 1, last_grads[min(step, micro_count - 1)], received
        )
        save_index = jnp.clip(step - phase_count + 1 + 2 * phase_index, 0, step_count - 1)
        hidden = lax.dynamic_index_in_dim(stack_hidden, save_index, 0, keepdims=False)
        queries = lax.dynamic_index_in_dim(stack_queries, save_index, 0, keepdims=False)
        key_rows = lax.dynamic_index_in_dim(stack_keys, save_index, 0, keepdims=False)
        value_rows = lax.dynamic_index_in_dim(stack_values, save_index, 0, keepdims=False)
        partial_sum = attention_back(
            gradient, queries, key_rows, value_rows, qkv_full, out_full, cosine, sine
        )
        d_normed = lax.psum(partial_sum.astype(jnp.bfloat16), "vocab").astype(jnp.float32)
        new_grad = (
            gradient.astype(jnp.float32) + norm_back(hidden.astype(jnp.float32), d_normed)
        ).astype(jnp.bfloat16)
        results.append(new_grad)
        received = from_behind(new_grad, "segment", -1)
    grad_owner = 0
    proj_part = jnp.zeros((encoded.shape[3], column_count), jnp.float32)
    for micro_index in range(micro_count):
        gradient = results[micro_index + phase_count - 1]
        columns = lax.dynamic_slice_in_dim(gradient, vocab_index * column_count, column_count, 1)
        d_image = jnp.dot(
            placings[micro_index].T, columns, preferred_element_type=jnp.float32
        ).astype(jnp.bfloat16)
        proj_part = proj_part + jnp.dot(
            encoded[micro_index, 0].T, d_image, preferred_element_type=jnp.float32
        )
    proj_part = jnp.where(phase_index == grad_owner, proj_part, jnp.zeros_like(proj_part))
    projector_grad = lax.psum_scatter(
        proj_part.astype(jnp.bfloat16), ("segment", "dp"), scatter_dimension=0, tiled=True
    ).astype(jnp.float32)
    return (loss, projector_grad)


def solution(mesh):
    placed = (
        P(None, "dp", None, None),
        P(None, "dp", None, None),
        P(),
        P(None, "dp"),
        P(None, "dp", None),
        P(None, "dp", None),
        P(),
        P(None, None, "vocab"),
        P(None, "vocab", None),
        P(None, "vocab"),
        P("segment", None, "dp", "vocab"),
        P("segment", "vocab", "dp"),
        P(("segment", "dp", "vocab"), None),
        P(None, ("segment", "dp", "vocab")),
    )
    return jax.shard_map(
        shards,
        mesh=mesh,
        in_specs=placed,
        out_specs=(P(), P(("segment", "dp"), "vocab")),
        check_vma=False,
    )
```

profile of v0, /device:TPU:2, one launch (start us, length us, event | category | flops | bytes accessed | tf_op | source)
XLA Modules:
  0.0 1881.3 jit_solution(6389302091463043287)
XLA Ops:
  8.1 11.3 fusion.523
  20.3 11.2 fusion.522
  31.5 6.1 fusion.58
  37.8 41.0 %all-reduce.15.cloned.1.call-done = bf16[72,1152]{1,0:T(8,128)(2,1)} async-done(((bf16[72,1152]{1,0:T(8,128)(2,1)}), bf16[72,1152]{1,0:T(8,128)(2,1)}) %all-reduce.15.cloned.1.call-update) | async-done | bytes 165904 | tf_op jit(solution)/shard_map/psum | solution.py:168
  80.1 6.1 fusion.59
  89.5 3.8 multiply_add_fusion
  93.8 32.4 %all-reduce.17.cloned.1.call-done = bf16[72,1152]{1,0:T(8,128)(2,1)} async-done(((bf16[72,1152]{1,0:T(8,128)(2,1)}), bf16[72,1152]{1,0:T(8,128)(2,1)}) %all-reduce.17.cloned.1.call-update) | async-done | bytes 165904 | tf_op jit(solution)/shard_map/psum | solution.py:168
  127.8 10.4 all_gather.34
  140.1 39.7 %all-gather.13.cloned.1.call-done = bf16[1,3,4096,512]{3,2,1,0:T(8,128)(2,1)} async-done(((bf16[1,3,256,512]{3,2,1,0:T(8,128)(2,1)}), bf16[1,3,4096,512]{3,2,1,0:T(8,128)(2,1)}) %all-gather.13.cloned.1.call-update) | async-done | bytes 12582928 | tf_op jit(solution)/shard_map/all_gather | solution.py:212
  179.8 5.8 slice_bitcast_fusion.1
  185.6 6.4 copy.152
  192.0 6.4 copy.151
  198.4 3.8 fusion.149
  204.2 3.0 fusion.97
  207.5 31.2 %all-gather.15.cloned.1.call-done = bf16[1,512,4096]{2,1,0:T(8,128)(2,1)} async-done(((bf16[1,512,256]{2,1,0:T(8,128)(2,1)}), bf16[1,512,4096]{2,1,0:T(8,128)(2,1)}) %all-gather.15.cloned.1.call-update) | async-done | bytes 4194320 | tf_op jit(solution)/shard_map/all_gather | solution.py:213
  238.7 3.9 convolution_convert_fusion.7
  242.6 42.1 %all-reduce.19.cloned.1.call-done = bf16[96,4096]{1,0:T(8,128)(2,1)} async-done(((bf16[96,4096]{1,0:T(8,128)(2,1)}), bf16[96,4096]{1,0:T(8,128)(2,1)}) %all-reduce.19.cloned.1.call-update) | async-done | bytes 786448 | tf_op jit(solution)/shard_map/psum | solution.py:252
  288.4 3.7 multiply_add_fusion.1
  292.4 15.8 collective-permute-done
  314.4 3.2 fusion.98
  319.7 43.2 %all-reduce.21.cloned.1.call-done = bf16[96,4096]{1,0:T(8,128)(2,1)} async-done(((bf16[96,4096]{1,0:T(8,128)(2,1)}), bf16[96,4096]{1,0:T(8,128)(2,1)}) %all-reduce.21.cloned.1.call-update) | async-done | bytes 786448 | tf_op jit(solution)/shard_map/psum | solution.py:252
  366.1 20.2 %collective-permute-done.1 = bf16[96,4096]{1,0:T(8,128)(2,1)S(1)} collective-permute-done((bf16[96,4096]{1,0:T(8,128)(2,1)S(1)}, bf16[96,4096]{1,0:T(8,128)(2,1)S(1)}, u32[]{:S(2)}, u32[]{:S(2)}) %collective-permute-start.1) | collective-permute-done | bytes 786464 | tf_op jit(solution)/shard_map/ppermute | solution.py:18
  390.8 3.2 fusion.99
  396.4 43.1 %all-reduce.23.cloned.1.call-done = bf16[96,4096]{1,0:T(8,128)(2,1)} async-done(((bf16[96,4096]{1,0:T(8,128)(2,1)}), bf16[96,4096]{1,0:T(8,128)(2,1)}) %all-reduce.23.cloned.1.call-update) | async-done | bytes 786448 | tf_op jit(solution)/shard_map/psum | solution.py:252
  441.7 27.4 %all-reduce.25.cloned.1.call-done = bf16[2,4,4096]{2,1,0:T(4,128)(2,1)} async-done(((bf16[2,4,4096]{2,1,0:T(4,128)(2,1)}), bf16[2,4,4096]{2,1,0:T(4,128)(2,1)}) %all-reduce.25.cloned.1.call-update) | async-done | bytes 65552 | tf_op jit(solution)/shard_map/psum | solution.py:23
  471.1 156.8 %all-gather.6 = f32[128,1,128]{2,1,0:T(1,128)S(1)} all-gather(f32[1,1,128]{2,1,0:T(1,128)S(1)} %get-tuple-element.328), channel_id=4, replica_groups=mesh['segment'=2,'dp'=16,'vocab'=4] {'segment','dp','vocab'}, dimensions={0}, use_global_device_ids=true | all-gather | bytes 66048 | tf_op jit(solution)/shard_map/all_gather | solution.py:27
  627.9 2.4 multiply_reduce_fusion
  635.3 150.3 %all-gather.5 = f32[128,1,128]{2,1,0:T(1,128)S(1)} all-gather(f32[1,1,128]{2,1,0:T(1,128)S(1)} %bitcast.588), channel_id=3, replica_groups=mesh['segment'=2,'dp'=16,'vocab'=4] {'segment','dp','vocab'}, dimensions={0}, use_global_device_ids=true | all-gather | bytes 66048 | tf_op jit(solution)/shard_map/all_gather | solution.py:27
  785.7 162.8 %all-gather.7 = f32[128,1,128]{2,1,0:T(1,128)S(1)} all-gather(f32[1,1,128]{2,1,0:T(1,128)S(1)} %bitcast.587), channel_id=5, replica_groups=mesh['segment'=2,'dp'=16,'vocab'=4] {'segment','dp','vocab'}, dimensions={0}, use_global_device_ids=true | all-gather | bytes 66048 | tf_op jit(solution)/shard_map/all_gather | solution.py:27
  948.5 170.0 %all-gather.8 = f32[128,1,128]{2,1,0:T(1,128)S(1)} all-gather(f32[1,1,128]{2,1,0:T(1,128)S(1)} %bitcast.586), channel_id=6, replica_groups=mesh['segment'=2,'dp'=16,'vocab'=4] {'segment','dp','vocab'}, dimensions={0}, use_global_device_ids=true | all-gather | bytes 66048 | tf_op jit(solution)/shard_map/all_gather | solution.py:27
  1119.1 184.3 %while.21 = (s32[]{:T(128)}, f32[128]{0:T(128)S(1)}, f32[128]{0:T(128)S(1)}, f32[128]{0:T(128)S(1)}, f32[128]{0:T(128)S(1)}, /*index=5*/f32[128,128]{1,0:T(8,128...) while((s32[]{:T(128)}, f32[128]{0:T(128)S(1)}, ...), condition=%wide.region_29.31_spmd, body=%wide.region_28.30_spmd.sunk | while | flops 1541 | bytes 8871 | solution.py:32
  1304.1 2.4 convolution_convert_fusion
  1314.1 128.5 %all-reduce.35.cloned.1.call-done = bf16[2,16,4,4096]{3,2,0,1:T(4,128)(2,1)} async-done(((bf16[2,16,4,4096]{3,2,0,1:T(4,128)(2,1)}), bf16[2,16,4,4096]{3,2,0,1:T(4,128)(2,1)}) %all-reduce.35.cloned.1.call-update) | async-done | bytes 1048592
  1442.5 2.1 dynamic-slice_bitcast_fusion
  1445.4 54.9 %all-reduce.27.cloned.1.call-done = bf16[2,4,4096]{2,1,0:T(4,128)(2,1)} async-done(((bf16[2,4,4096]{2,1,0:T(4,128)(2,1)}), bf16[2,4,4096]{2,1,0:T(4,128)(2,1)}) %all-reduce.27.cloned.1.call-update) | async-done | bytes 65552 | tf_op jit(solution)/shard_map/psum | solution.py:298
  1503.2 3.9 fusion.136
  1508.7 3.6 fusion.43
  1512.3 3.6 convolution_add_fusion.5
  1515.9 4.5 fusion.18
  1522.1 42.4 %all-reduce.29.cloned.1.call-done = bf16[96,4096]{1,0:T(8,128)(2,1)} async-done(((bf16[96,4096]{1,0:T(8,128)(2,1)}), bf16[96,4096]{1,0:T(8,128)(2,1)}) %all-reduce.29.cloned.1.call-update) | async-done | bytes 786448 | tf_op jit(solution)/shard_map/psum | solution.py:327
  1564.5 2.0 multiply_reduce_fusion.2
  1568.0 4.4 collective-permute-start.2
  1576.0 12.9 collective-permute-done.2
  1588.9 3.6 fusion.133
  1593.5 2.1 fusion.115
  1595.6 2.2 fusion.117
  1597.7 2.0 fusion.128
  1601.1 3.6 fusion.41
  1604.7 3.6 convolution_add_fusion.3
  1608.4 4.5 fusion.19
  1612.9 44.2 %all-reduce.31.cloned.1.call-done = bf16[96,4096]{1,0:T(8,128)(2,1)} async-done(((bf16[96,4096]{1,0:T(8,128)(2,1)}), bf16[96,4096]{1,0:T(8,128)(2,1)}) %all-reduce.31.cloned.1.call-update) | async-done | bytes 786448 | tf_op jit(solution)/shard_map/psum | solution.py:327
  1658.6 2.7 fusion.69
  1661.3 4.7 collective-permute-start.3
  1667.8 14.7 collective-permute-done.3
  1682.6 4.0 fusion.130
  1691.7 3.6 fusion.45
  1695.2 3.6 convolution_add_fusion.1
  1698.9 4.5 fusion.20
  1704.7 4.0 fusion.139
  1708.8 39.8 %all-reduce.33.cloned.1.call-done = bf16[96,4096]{1,0:T(8,128)(2,1)} async-done(((bf16[96,4096]{1,0:T(8,128)(2,1)}), bf16[96,4096]{1,0:T(8,128)(2,1)}) %all-reduce.33.cloned.1.call-update) | async-done | bytes 786448 | tf_op jit(solution)/shard_map/psum | solution.py:327
  1750.1 2.5 convert_element_type.625
  1752.6 5.3 fusion.47
  1757.8 98.2 %fusion = bf16[40,1024]{1,0:T(8,128)(2,1)S(1)} fusion(bf16[1152,1024]{1,0:T(8,128)(2,1)} %fusion.47), kind=kCustom, calls=%all-reduce-scatter | all-reduce-scatter fusion | flops 1310721 | bytes 2441728
  1865.6 5.3 collective-permute-done.7
  (676 shorter events, 268.3 us)
Async XLA Ops:
  8.0 119.2 %copy-start = (bf16[1152,1024]{1,0:T(8,128)(2,1)S(1)}, bf16[1152,1024]{1,0:T(8,128)(2,1)}, u32[]{:S(2)}) copy-start(bf16[1152,1024]{1,0:T(8,128)(2,1)} %param.27) | copy-start | bytes 7077892
  8.0 11.4 copy-start.16
  8.0 70.8 %all-reduce.15.cloned.1.call-start = ((), (), s32[]{:S(2)}) async-start(), calls=%async_computation | async-start | bytes 331776 | tf_op jit(solution)/shard_map/psum | solution.py:168
  37.6 88.5 %all-reduce.17.cloned.1.call-start = ((), (), s32[]{:S(2)}) async-start(), calls=%async_computation.1 | async-start | bytes 331776 | tf_op jit(solution)/shard_map/psum | solution.py:168
  80.1 7.4 copy-start.55
  80.1 8.7 copy-start.56
  80.1 13.2 copy-start.57
  86.2 93.6 %all-gather.13.cloned.1.call-start = ((), (), s32[]{:S(2)}) async-start(), calls=%async_computation.2 | async-start | bytes 13369344 | tf_op jit(solution)/shard_map/all_gather | solution.py:212
  86.8 51.3 %copy-start.63 = (bf16[4096]{0:T(1024)(128)(2,1)S(1)}, bf16[4096]{0:T(1024)(128)(2,1)}, u32[]{:S(2)}) copy-start(bf16[4096]{0:T(1024)(128)(2,1)} %param.20) | copy-start | bytes 24580
  86.8 151.8 %all-gather.15.cloned.1.call-start = ((), (), s32[]{:S(2)}) async-start(), calls=%async_computation.3 | async-start | bytes 4456448 | tf_op jit(solution)/shard_map/all_gather | solution.py:213
  87.4 197.3 %all-reduce.19.cloned.1.call-start = ((), (), s32[]{:S(2)}) async-start(), calls=%async_computation.4 | async-start | bytes 1572864 | tf_op jit(solution)/shard_map/psum | solution.py:252
  88.8 51.2 %copy-start.60 = (pred[36]{0:T(512)(128)(4,1)}, pred[36]{0:T(512)(128)(4,1)S(1)}, u32[]{:S(2)}) copy-start(pred[36]{0:T(512)(128)(4,1)S(1)} %broadcast_compare_fusion) | copy-start | bytes 112
  140.1 144.7 %copy-start.9 = (bf16[96,4096]{1,0:T(8,128)(2,1)}, bf16[96,4096]{1,0:T(8,128)(2,1)S(1)}, u32[]{:S(2)}) copy-start(bf16[96,4096]{1,0:T(8,128)(2,1)S(1)} %get-tuple-element.347) | copy-start | bytes 2359300
  198.4 3.8 copy-start.6
  207.2 35.3 %copy-start.47 = (bf16[96,512]{1,0:T(8,128)(2,1)}, bf16[96,512]{1,0:T(8,128)(2,1)S(1)}, u32[]{:S(2)}) copy-start(bf16[96,512]{1,0:T(8,128)(2,1)S(1)} %fusion.97) | copy-start | bytes 294916
  242.6 120.3 %all-reduce.21.cloned.1.call-start = ((), (), s32[]{:S(2)}) async-start(), calls=%async_computation.5 | async-start | bytes 1572864 | tf_op jit(solution)/shard_map/psum | solution.py:252
  284.7 23.4 %copy-start.62 = (bf16[2,1,96,4096]{3,2,1,0:T(8,128)(2,1)S(1)}, bf16[2,1,96,4096]{3,2,1,0:T(8,128)(2,1)}, u32[]{:S(2)}) copy-start(bf16[2,1,96,4096]{3,2,1,0:T(8,128)(2,1)} %param.19) | copy-start | bytes 4718596
  286.2 23.7 %copy-start.4 = (bf16[512,4096]{1,0:T(8,128)(2,1)S(1)}, bf16[512,4096]{1,0:T(8,128)(2,1)}, u32[]{:S(2)}) copy-start(bf16[512,4096]{1,0:T(8,128)(2,1)} %copy.152) | copy-start | bytes 12582916
  286.2 21.9 %collective-permute-start = (bf16[96,4096]{1,0:T(8,128)(2,1)S(1)}, bf16[96,4096]{1,0:T(8,128)(2,1)S(1)}, u32[]{:S(2)}, u32[]{:S(2)}) collective-permute-start(bf16[96,4096]{1,0:T(8,128)(2,1)S(1)} %fusion.72), channel_id=1, source_target_pairs={{0,64},{1,65},{2,66},{3,67},{4,68},{5,69},{6,70},{7,71},{8,72},{9,... | collective-permute-start | bytes 2359304 | tf_op jit(solution)/shard_map/ppermute | solution.py:18
  309.9 53.0 %copy-start.10 = (bf16[96,4096]{1,0:T(8,128)(2,1)}, bf16[96,4096]{1,0:T(8,128)(2,1)S(1)}, u32[]{:S(2)}) copy-start(bf16[96,4096]{1,0:T(8,128)(2,1)S(1)} %get-tuple-element.264) | copy-start | bytes 2359300
  319.7 119.9 %all-reduce.23.cloned.1.call-start = ((), (), s32[]{:S(2)}) async-start(), calls=%async_computation.6 | async-start | bytes 1572864 | tf_op jit(solution)/shard_map/psum | solution.py:252
  362.9 23.7 %copy-start.5 = (bf16[512,4096]{1,0:T(8,128)(2,1)S(1)}, bf16[512,4096]{1,0:T(8,128)(2,1)}, u32[]{:S(2)}) copy-start(bf16[512,4096]{1,0:T(8,128)(2,1)} %copy.152) | copy-start | bytes 12582916
  364.4 21.8 %collective-permute-start.1 = (bf16[96,4096]{1,0:T(8,128)(2,1)S(1)}, bf16[96,4096]{1,0:T(8,128)(2,1)S(1)}, u32[]{:S(2)}, u32[]{:S(2)}) collective-permute-start(bf16[96,4096]{1,0:T(8,128)(2,1)S(1)} %fusion.75), channel_id=1, source_target_pairs={{0,64},{1,65},{2,66},{3,67},{4,68},{5,69},{6,70},{7,71},{8,72},{9,... | collective-permute-start | bytes 2359304 | tf_op jit(solution)/shard_map/ppermute | solution.py:18
  396.1 74.6 %copy-start.58 = (s32[2,16]{1,0:T(2,128)S(1)}, s32[2,16]{1,0:T(2,128)}, u32[]{:S(2)}) copy-start(s32[2,16]{1,0:T(2,128)} %param.24) | copy-start | bytes 388
  396.1 74.9 %copy-start.36 = (bf16[128,256]{1,0:T(8,128)(2,1)S(1)}, bf16[128,256]{1,0:T(8,128)(2,1)}, u32[]{:S(2)}) copy-start(bf16[128,256]{1,0:T(8,128)(2,1)} %param.31) | copy-start | bytes 196612
  396.1 73.0 %all-reduce.25.cloned.1.call-start = ((), (), s32[]{:S(2)}) async-start(), calls=%async_computation.7 | async-start | bytes 131072 | tf_op jit(solution)/shard_map/psum | solution.py:23
  441.6 186.2 %all-gather.17.cloned.1.call-start = ((), (), s32[]{:S(2)}) async-start(), calls=%async_computation.12 | async-start | bytes 1114112 | tf_op jit(solution)/shard_map/all_gather | solution.py:268
  470.6 971.9 %all-reduce.35.cloned.1.call-start = ((), (), s32[]{:S(2)}) async-start(), calls=%async_computation.13 | async-start | bytes 2097152
  785.7 332.8 %copy-start.52 = (f32[128,1,128]{2,1,0:T(1,128)}, f32[128,1,128]{2,1,0:T(1,128)S(1)}, u32[]{:S(2)}) copy-start(f32[128,1,128]{2,1,0:T(1,128)S(1)} %all-gather.5) | copy-start | bytes 196612
  948.5 170.0 %copy-start.53 = (f32[128,1,128]{2,1,0:T(1,128)}, f32[128,1,128]{2,1,0:T(1,128)S(1)}, u32[]{:S(2)}) copy-start(f32[128,1,128]{2,1,0:T(1,128)S(1)} %all-gather.7) | copy-start | bytes 196612
  1308.0 5.4 copy-start.18
  1308.0 5.4 copy-start.24
  1308.0 5.4 copy-start.26
  1308.0 5.4 copy-start.32
  1308.0 5.4 copy-start.34
  1308.0 5.5 copy-start.20
  1308.0 5.5 copy-start.22
  1308.1 5.5 copy-start.28
  1308.1 5.5 copy-start.30
  1309.8 190.5 %copy-start.35 = (bf16[2,4,4096]{2,1,0:T(4,128)(2,1)S(1)}, bf16[2,4,4096]{2,1,0:T(4,128)(2,1)}, u32[]{:S(2)}) copy-start(bf16[2,4,4096]{2,1,0:T(4,128)(2,1)} %all-reduce.25.cloned.1.call-done) | copy-start | bytes 196612
  1309.8 190.5 %all-reduce.27.cloned.1.call-start = ((), (), s32[]{:S(2)}) async-start(), calls=%async_computation.8 | async-start | bytes 131072 | tf_op jit(solution)/shard_map/psum | solution.py:298
  1313.6 187.7 %copy-start.39 = (bf16[3,96,4,128]{3,1,2,0:T(8,128)(2,1)}, bf16[3,96,4,128]{3,1,2,0:T(8,128)(2,1)S(1)}, u32[]{:S(2)}) copy-start(bf16[3,96,4,128]{3,1,2,0:T(8,128)(2,1)S(1)} %maximum_maximum_fusion) | copy-start | bytes 884740
  1313.8 194.4 %copy-start.42 = (bf16[3,96,4,128]{3,1,2,0:T(8,128)(2,1)}, bf16[3,96,4,128]{3,1,2,0:T(8,128)(2,1)S(1)}, u32[]{:S(2)}) copy-start(bf16[3,96,4,128]{3,1,2,0:T(8,128)(2,1)S(1)} %maximum_maximum_fusion.1) | copy-start | bytes 884740
  1444.6 119.9 %all-reduce.29.cloned.1.call-start = ((), (), s32[]{:S(2)}) async-start(), calls=%async_computation.9 | async-start | bytes 1572864 | tf_op jit(solution)/shard_map/psum | solution.py:327
  1502.3 4.9 copy-start.43
  1503.2 3.9 copy-start.13
  1503.2 4.2 copy-start.40
  1520.4 136.7 %all-reduce.31.cloned.1.call-start = ((), (), s32[]{:S(2)}) async-start(), calls=%async_computation.10 | async-start | bytes 1572864 | tf_op jit(solution)/shard_map/psum | solution.py:327
  1522.1 44.4 %copy-start.14 = (bf16[96,4096]{1,0:T(8,128)(2,1)S(1)}, bf16[96,4096]{1,0:T(8,128)(2,1)}, u32[]{:S(2)}) copy-start(bf16[96,4096]{1,0:T(8,128)(2,1)} %copy-done.13) | copy-start | bytes 2359300
  1568.0 21.0 %collective-permute-start.2 = (bf16[96,4096]{1,0:T(8,128)(2,1)}, bf16[96,4096]{1,0:T(8,128)(2,1)}, u32[]{:S(2)}, u32[]{:S(2)}) collective-permute-start(bf16[96,4096]{1,0:T(8,128)(2,1)} %fusion.66), channel_id=1, source_target_pairs={{64,0},{65,1},{66,2},{67,3},{68,4},{69,5},{70,6},{71,7},{72,8},{73... | collective-permute-start | bytes 2359304 | tf_op jit(solution)/shard_map/ppermute | solution.py:18
  1576.0 16.6 copy-start.37
  1576.0 16.6 copy-start.45
  1604.7 3.7 copy-start.50
  1612.9 135.8 %all-reduce.33.cloned.1.call-start = ((), (), s32[]{:S(2)}) async-start(), calls=%async_computation.11 | async-start | bytes 1572864 | tf_op jit(solution)/shard_map/psum | solution.py:327
  1661.3 21.2 %collective-permute-start.3 = (bf16[96,4096]{1,0:T(8,128)(2,1)}, bf16[96,4096]{1,0:T(8,128)(2,1)}, u32[]{:S(2)}, u32[]{:S(2)}) collective-permute-start(bf16[96,4096]{1,0:T(8,128)(2,1)} %fusion.69), channel_id=1, source_target_pairs={{64,0},{65,1},{66,2},{67,3},{68,4},{69,5},{70,6},{71,7},{72,8},{73... | collective-permute-start | bytes 2359304 | tf_op jit(solution)/shard_map/ppermute | solution.py:18
  1682.6 4.0 copy-start.12
  1682.6 4.0 copy-start.44
  1682.6 4.9 copy-start.41
  1752.6 119.8 %copy-start.1 = (bf16[1152,1024]{1,0:T(8,128)(2,1)S(1)}, bf16[1152,1024]{1,0:T(8,128)(2,1)}, u32[]{:S(2)}) copy-start(bf16[1152,1024]{1,0:T(8,128)(2,1)} %param.27) | copy-start | bytes 7077892
  1757.8 105.9 %copy-start.59 = (u32[128]{0:T(128)S(1)}, u32[128]{0:T(128)}, u32[]{:S(2)}) copy-start(u32[128]{0:T(128)} %constant.236) | copy-start | bytes 1540
  1856.0 14.9 collective-permute-start.6
  1857.9 13.0 collective-permute-start.5
  1859.9 11.1 collective-permute-start.4
  1861.8 9.1 collective-permute-start.7
  (23 other events, 60.5 us)
Sparse Core Ops, SparseCore 0:
  37.8 40.9 all-reduce.14
  86.4 39.7 all-reduce.16
  242.7 41.9 all-reduce.18
  319.8 43.1 all-reduce.20
  396.2 43.2 all-reduce.22
  442.3 26.6 all-reduce.24
  1444.7 55.5 all-reduce.26
  1520.5 43.8 all-reduce.28
  1613.0 44.1 all-reduce.30
  1703.5 45.0 all-reduce.32
Sparse Core Ops, SparseCore 1:
  88.9 90.9 all-gather.12
  181.8 56.8 all-gather.14
  470.7 44.8 all-gather.16
  1309.8 132.6 all-reduce.34
where the time goes:
time: 1900 us; the launch traced here: 1880 us
  blocking collectives  748 us (39%)
  waiting for transfers between devices  680 us (36%)
  other arithmetic  223 us (12%)
  matrix products  126 us (7%)
  local copies, waits for them, and re-layouts  60.1 us (3%)
  starting transfers between devices  20.6 us (1%)
  between operations  19.9 us (1%)
    all_gather x4, blocking collectives, merged(): gathered = jax.tree.map(lambda a: lax.all_gather(a, axis), part)  640 us
    unnamed x19, waiting for transfers between devices  135 us
    psum x3, waiting for transfers between devices, shards(): lax.psum(partial_out.astype(jnp.bfloat16), 'vocab').astype(jnp.float32)  128 us
    psum x3, waiting for transfers between devices, shards(): lax.psum(partial_sum.astype(jnp.bfloat16), 'vocab').astype(jnp.float32)  126 us
    unnamed x1, blocking collectives  98.2 us
    add x127, other arithmetic, join_parts(): sum_student = earlier[0] + later[0]  91.7 us
    add x127, other arithmetic, join_parts(): cross = earlier[3] * factor_early + later[3] * factor_late  89.8 us
    psum x2, waiting for transfers between devices, encode_rows(): lax.psum(jnp.dot(inner, enc_down[layer], preferred_element_type=jnp.float...  73.4 us
  transfers between devices with their start and end apart: 22, of which 18 were waited for; matrix products, arithmetic and copies ran while one was open for 3% of the time, Pallas kernels for 0%

commit v1 on v0

v1 whole, which is shorter than its diff:
```python
import jax
import jax.numpy as jnp
from jax import lax
from jax.sharding import PartitionSpec as P

HD = 128
MASKED = 4
RATIOS = 8

epsilon = 1e-06
rope_base = 500000.0

LINE = ("vocab", "segment")
ALL = ("segment", "dp", "vocab")
f32 = jnp.float32
bf16 = jnp.bfloat16


def dot(a, b):
    return jnp.dot(a, b, preferred_element_type=f32)


def dot_nt(a, b):
    return lax.dot_general(a, b, (((1,), (1,)), ((), ())), preferred_element_type=f32)


def dot_tn(a, b):
    return lax.dot_general(a, b, (((0,), (0,)), ((), ())), preferred_element_type=f32)


def swap(block, axis, mask):
    return lax.ppermute(block, axis, [(i, i ^ mask) for i in range(lax.axis_size(axis))])


def exchange(chunks, axes):
    return lax.all_to_all(chunks, axes, 0, 0, tiled=True)


def spread(block, axes):
    size = lax.axis_size(axes)
    return exchange(jnp.broadcast_to(block[None], (size,) + block.shape), axes)


def inverse_rms(values_in):
    return lax.rsqrt(jnp.mean(values_in * values_in, axis=-1, keepdims=True) + epsilon)


def norm_rows(values_in):
    return values_in * inverse_rms(values_in)


def layer_norm(values_in):
    centred = values_in - jnp.mean(values_in, axis=-1, keepdims=True)
    return centred * lax.rsqrt(jnp.mean(centred * centred, axis=-1, keepdims=True) + epsilon)


def norm_back(values_in, cotangent):
    factor = inverse_rms(values_in)
    return factor * cotangent - values_in * factor**3 * jnp.mean(
        cotangent * values_in, axis=-1, keepdims=True
    )


def rope_tables(positions):
    halfway = HD // 2
    inverse = rope_base ** (-2.0 * jnp.arange(halfway, dtype=f32) / HD)
    angles = positions.astype(f32)[..., None] * inverse
    return jnp.cos(angles), jnp.sin(angles)


def rotate(values_in, cosine, sine):
    halfway = values_in.shape[-1] // 2
    first_half = values_in[..., :halfway]
    second_half = values_in[..., halfway:]
    return jnp.concatenate(
        [first_half * cosine - second_half * sine, second_half * cosine + first_half * sine],
        axis=-1,
    )


def encode_rows(current, enc_up, enc_down):
    for layer in range(enc_up.shape[0]):
        normed = layer_norm(current.astype(f32)).astype(bf16)
        inner = jax.nn.gelu(dot(normed, enc_up[layer]), approximate=True).astype(bf16)
        part = dot(inner, enc_down[layer]).astype(bf16)
        others = [swap(part, "vocab", mask).astype(f32) for mask in (1, 2, 3)]
        summed = (part.astype(f32) + others[0]) + (others[1] + others[2])
        current = (current.astype(f32) + summed).astype(bf16)
    return current


def scores_of(queries, keys):
    scores = jnp.einsum("sqhd,skhd->shqk", queries, keys, preferred_element_type=f32)
    return jax.nn.softmax(scores * HD ** (-0.5), axis=-1)


def mix(probs, values):
    return jnp.einsum(
        "shqk,skhd->sqhd", probs.astype(bf16), values, preferred_element_type=f32
    ).astype(bf16)


def score_back(probs, values, d_mixed):
    d_probs = jnp.einsum("sqhd,skhd->shqk", d_mixed, values, preferred_element_type=f32)
    d_probs = d_probs.astype(bf16).astype(f32)
    d_scores = probs * (d_probs - jnp.sum(probs * d_probs, axis=-1, keepdims=True))
    return (d_scores * HD ** (-0.5)).astype(bf16)


def shards(
    patches,
    text_embed,
    mask_embed,
    image_counts,
    image_order,
    masked_positions,
    ratio_index,
    enc_up,
    enc_down,
    projector,
    lang_qkv,
    lang_out,
    head_weight,
    teacher_logits,
):
    segment = lax.axis_index("segment")
    dp_index = lax.axis_index("dp")
    place = lax.axis_index("vocab") * 2 + segment
    line = lax.axis_size(LINE)
    dp_size = lax.axis_size("dp")
    micro = text_embed.shape[0]
    seq_len, width = text_embed.shape[2:]
    slots = patches.shape[2]
    depth = patches.shape[3]
    per_image = slots // image_order.shape[2]

    shard = jnp.concatenate(
        [lang_qkv[0], jnp.transpose(lang_out[0])[None]], axis=0
    )
    half = shard.shape[2] // 2
    rows_here = shard.shape[1]
    low, high = shard[:, :, :half], shard[:, :, half:]
    keep = jnp.where(segment == 0, low, high)
    give = jnp.where(segment == 0, high, low)
    got = swap(give, "segment", 1)
    sections = (
        jnp.where(segment == 0, keep, got),
        jnp.where(segment == 0, got, keep),
    )
    weights = [
        lax.all_gather(
            jnp.transpose(part, (1, 0, 2)).reshape(rows_here, 4 * half), "dp", axis=0, tiled=True
        )
        for part in sections
    ]
    w_qkv = [w[:, : 3 * half] for w in weights]
    w_out = [w[:, 3 * half :] for w in weights]
    heads = half // HD

    encoded = encode_rows(patches.reshape(micro * slots, depth), enc_up, enc_down)
    image_cols = dot(encoded, projector).astype(bf16)
    images = lax.all_gather(image_cols, "vocab", axis=1, tiled=True)

    slot_ids = jnp.arange(slots, dtype=jnp.int32)
    cell_ids = jnp.arange(seq_len, dtype=jnp.int32)
    image_of = slot_ids // per_image
    placings = []
    picks = []
    sequences = []
    for index in range(micro):
        target = jnp.take(image_order[index, 0], image_of) * per_image + slot_ids % per_image
        live = image_of < image_counts[index, 0]
        matches = (target[None, :] == slot_ids[:, None]) & live[None, :]
        placing = matches.astype(bf16)
        placings.append(placing)
        placed = dot(placing, images[index * slots : (index + 1) * slots]).astype(bf16)
        top = jnp.where(
            jnp.any(matches, axis=1)[:, None], placed, text_embed[index, 0, :slots]
        )
        pick = masked_positions[index, 0][:, None] == cell_ids[None, :]
        picks.append(pick.astype(bf16))
        bottom = jnp.where(
            jnp.any(pick, axis=0)[slots:, None], mask_embed[None, :], text_embed[index, 0, slots:]
        )
        sequences += [top, bottom]
    hidden0 = jnp.concatenate(sequences, axis=0)
    tokens = micro * seq_len
    chunk_rows = tokens // line
    pick_all = jnp.zeros((micro * MASKED, tokens), bf16)
    for index in range(micro):
        pick_all = lax.dynamic_update_slice(
            pick_all, picks[index], (index * MASKED, index * seq_len)
        )

    cosine, sine = (t[None, :, None, :] for t in rope_tables(cell_ids))
    mask_cos, mask_sin = (
        t.reshape(micro, MASKED, 1, HD // 2) for t in rope_tables(masked_positions[:, 0])
    )

    def project(hidden, w):
        normed = norm_rows(hidden.astype(f32)).astype(bf16)
        out = dot(normed, w).reshape(micro, seq_len, 3, heads, HD)
        return out[:, :, 0], out[:, :, 1], out[:, :, 2]

    def own_rows(array):
        return lax.dynamic_slice_in_dim(array, place * chunk_rows, chunk_rows, 0)

    def sum_rows(partial):
        parts = exchange(partial.astype(bf16).reshape(line, chunk_rows, width), LINE)
        return jnp.sum(parts.astype(f32), axis=0)

    q, k, v = project(hidden0, w_qkv[0])
    q0 = rotate(q, cosine, sine).astype(bf16)
    k0 = rotate(k, cosine, sine).astype(bf16)
    v0 = v.astype(bf16)
    probs0 = scores_of(q0, k0)
    mixed = mix(probs0, v0).reshape(tokens, half)
    mine = (own_rows(hidden0).astype(f32) + sum_rows(dot_nt(mixed, w_out[0]))).astype(bf16)
    hidden1 = spread(mine, LINE).reshape(tokens, width)

    q, k, v = project(hidden1, w_qkv[1])
    q = jnp.einsum(
        "smt,sthd->smhd", jnp.stack(picks).astype(f32), q, precision=lax.Precision.HIGHEST
    )
    q1 = rotate(q, mask_cos, mask_sin).astype(bf16)
    k1 = rotate(k, cosine, sine).astype(bf16)
    v1 = v.astype(bf16)
    probs1 = scores_of(q1, k1)
    mixed = mix(probs1, v1).reshape(micro * MASKED, half)
    partial = dot_nt(mixed, w_out[1]).astype(bf16)
    cols = width // line
    masked_rows = micro * MASKED
    parts = exchange(
        jnp.transpose(partial.reshape(masked_rows, line, cols), (1, 0, 2)), LINE
    )
    picked = lax.dynamic_slice_in_dim(dot(pick_all, hidden1), place * cols, cols, 1)
    last = (picked + jnp.sum(parts.astype(f32), axis=0)).astype(bf16)

    all_rows = spread(last, ALL).reshape(2, dp_size, 4, masked_rows, cols)
    all_rows = jnp.transpose(all_rows, (1, 3, 2, 0, 4)).reshape(dp_size * masked_rows, width)
    row_count = all_rows.shape[0]
    final = norm_rows(all_rows.astype(f32)).astype(bf16)
    logits = dot_nt(final, head_weight)

    teacher = (
        jnp.transpose(teacher_logits.reshape(micro, dp_size, MASKED, -1), (1, 0, 2, 3))
        .reshape(row_count, -1)
        .astype(f32)
    )
    top = jnp.max(teacher, axis=1)
    powers = jnp.exp(teacher - top[:, None])
    stats = jnp.stack(
        [
            jnp.sum(jnp.exp(logits), axis=1),
            top,
            jnp.sum(powers, axis=1),
            jnp.sum(powers * (teacher - logits), axis=1),
        ]
    )
    stats = spread(stats, ALL).reshape(-1, 4, row_count)
    sum_student = jnp.sum(stats[:, 0], axis=0)
    top_all = jnp.max(stats[:, 1], axis=0)
    scale = jnp.exp(stats[:, 1] - top_all[None])
    sum_teacher = jnp.sum(stats[:, 2] * scale, axis=0)
    cross = jnp.sum(stats[:, 3] * scale, axis=0)
    norm_student = jnp.log(sum_student)
    norm_teacher = top_all + jnp.log(sum_teacher)
    divergence = cross / sum_teacher - norm_teacher + norm_student
    ratio = RATIOS / ratio_index.astype(f32)
    row_weights = jnp.repeat(jnp.transpose(ratio), MASKED, axis=1).reshape(-1)
    total = micro * dp_size
    loss = jnp.sum(row_weights * divergence) / total
    d_logits = (
        (row_weights / total)[:, None]
        * (jnp.exp(logits - norm_student[:, None]) - jnp.exp(teacher - norm_teacher[:, None]))
    ).astype(bf16)
    d_final = dot(d_logits, head_weight).astype(bf16)
    d_final = jnp.transpose(
        d_final.reshape(dp_size, masked_rows, 4, 2, cols), (3, 0, 2, 1, 4)
    ).reshape(-1, masked_rows, cols)
    d_own = jnp.sum(exchange(d_final, ALL).astype(f32), axis=0).astype(bf16)
    d_own = jnp.transpose(spread(d_own, LINE).reshape(line, masked_rows, cols), (1, 0, 2)).reshape(
        masked_rows, width
    )
    rows = lax.dynamic_slice_in_dim(all_rows, dp_index * masked_rows, masked_rows, 0)
    grad_rows = norm_back(rows.astype(f32), d_own.astype(f32)).astype(bf16)

    d_mixed = dot(grad_rows, w_out[1]).astype(bf16).reshape(micro, MASKED, heads, HD)
    d_scores = score_back(probs1, v1, d_mixed)
    d_q = jnp.einsum("shqk,skhd->sqhd", d_scores, k1, preferred_element_type=f32)
    d_k = jnp.einsum("shqk,sqhd->skhd", d_scores, q1, preferred_element_type=f32)
    d_v = jnp.einsum("shqk,sqhd->skhd", probs1.astype(bf16), d_mixed, preferred_element_type=f32)
    d_q = rotate(d_q.astype(bf16).astype(f32), mask_cos, -mask_sin).astype(bf16)
    d_q = dot_tn(pick_all, d_q.reshape(masked_rows, half)).astype(bf16)
    d_k = rotate(d_k.astype(bf16).astype(f32), cosine, -sine).astype(bf16).reshape(tokens, half)
    d_v = d_v.astype(bf16).reshape(tokens, half)
    d_normed = sum_rows(dot_nt(jnp.concatenate([d_q, d_k, d_v], axis=1), w_qkv[1]))
    own_pick = lax.dynamic_slice_in_dim(pick_all, place * chunk_rows, chunk_rows, 1)
    grad_own = dot_tn(own_pick, grad_rows)
    grad_own = (grad_own + norm_back(own_rows(hidden1).astype(f32), d_normed)).astype(bf16)
    grad = spread(grad_own, LINE).reshape(tokens, width)

    d_mixed = dot(grad, w_out[0]).astype(bf16).reshape(micro, seq_len, heads, HD)
    d_scores = score_back(probs0, v0, d_mixed)
    d_q = jnp.einsum("shqk,skhd->sqhd", d_scores[:, :, :slots], k0, preferred_element_type=f32)
    d_k = jnp.einsum("shqk,sqhd->skhd", d_scores[..., :slots], q0, preferred_element_type=f32)
    d_v = jnp.einsum(
        "shqk,sqhd->skhd", probs0[..., :slots].astype(bf16), d_mixed, preferred_element_type=f32
    )
    cos_top, sin_top = cosine[:, :slots], sine[:, :slots]
    d_q = rotate(d_q.astype(bf16).astype(f32), cos_top, -sin_top).astype(bf16)
    d_k = rotate(d_k.astype(bf16).astype(f32), cos_top, -sin_top).astype(bf16)
    cells = micro * slots
    d_all = jnp.concatenate(
        [d_q.reshape(cells, half), d_k.reshape(cells, half), d_v.astype(bf16).reshape(cells, half)],
        axis=1,
    )
    partial = dot_nt(d_all, w_qkv[0]).astype(bf16)
    top_hidden = jnp.concatenate(
        [hidden0[i * seq_len : i * seq_len + slots] for i in range(micro)], axis=0
    ).astype(f32)
    top_grad = jnp.concatenate(
        [grad[i * seq_len : i * seq_len + slots] for i in range(micro)], axis=0
    )
    along = jnp.mean(partial.astype(f32) * top_hidden, axis=1)
    along_high = along.astype(bf16)
    along_low = (along - along_high.astype(f32)).astype(bf16)
    extra = jnp.zeros((8, cols), bf16)
    extra = extra.at[0, :cells].set(along_high).at[1, :cells].set(along_low)
    chunks = jnp.concatenate(
        [
            jnp.transpose(partial.reshape(cells, line, cols), (1, 0, 2)),
            jnp.broadcast_to(extra[None], (line,) + extra.shape),
        ],
        axis=1,
    )
    summed = jnp.sum(exchange(chunks, LINE).astype(f32), axis=0)
    d_normed = summed[:cells]
    along = (summed[cells, :cells] + summed[cells + 1, :cells])[:, None]
    factor = inverse_rms(top_hidden)
    hidden_cols = lax.dynamic_slice_in_dim(top_hidden, place * cols, cols, 1)
    grad_cols = lax.dynamic_slice_in_dim(top_grad, place * cols, cols, 1).astype(f32)
    new_grad = (grad_cols + factor * d_normed - hidden_cols * factor**3 * along).astype(bf16)
    d_image = jnp.concatenate(
        [
            dot_tn(placings[i], new_grad[i * slots : (i + 1) * slots]).astype(bf16)
            for i in range(micro)
        ],
        axis=0,
    )
    proj_part = dot_tn(encoded, d_image).astype(bf16)
    owners = 2 * dp_size
    parts = exchange(proj_part.reshape(owners, depth // owners, cols), ("segment", "dp"))
    parts = jnp.sum(parts.astype(f32).reshape(2, dp_size, depth // owners, cols), axis=1)
    projector_grad = jnp.transpose(parts, (1, 0, 2)).reshape(depth // owners, 2 * cols)
    return (loss, projector_grad)


def solution(mesh):
    placed = (
        P(None, "dp", None, None),
        P(None, "dp", None, None),
        P(),
        P(None, "dp"),
        P(None, "dp", None),
        P(None, "dp", None),
        P(),
        P(None, None, "vocab"),
        P(None, "vocab", None),
        P(None, "vocab"),
        P("segment", None, "dp", "vocab"),
        P("segment", "vocab", "dp"),
        P(("segment", "dp", "vocab"), None),
        P(None, ("segment", "dp", "vocab")),
    )
    return jax.shard_map(
        shards,
        mesh=mesh,
        in_specs=placed,
        out_specs=(P(), P(("segment", "dp"), "vocab")),
        check_vma=False,
    )
```

time: 1900 us -> 432 us (0.23)
  blocking collectives: 748 us -> 56.7 us
  waiting for transfers between devices: 680 us -> 152 us
  other arithmetic: 223 us -> 33.8 us
  matrix products: 126 us -> 58.6 us
  starting transfers between devices: 20.6 us -> 55.4 us
    all_gather x5 -> x1, blocking collectives: 650 us -> 10.1 us  [shards(): images = lax.all_gather(image_cols, 'vocab', axis=1, tiled=True)]
    psum x10 -> x0, waiting for transfers between devices: 411 us -> none  [the longest x3 128 us: shards(): lax.psum(partial_out.astype(jnp.bfloat16), 'vocab').astype(jnp.float32)]
    add x256 -> x2, other arithmetic: 189 us -> 7.43 us  [the longest x1 7.43 us: shards(): jnp.take(image_order[index, 0], image_of) * per_image + slot_ids % per_image]
    unnamed x19 -> x2, waiting for transfers between devices: 135 us -> 0.03 us
    unnamed x1 -> x0, blocking collectives: 98.2 us -> none
    all_to_all x0 -> x9, waiting for transfers between devices: none -> 98.1 us  [exchange(): return lax.all_to_all(chunks, axes, 0, 0, tiled=True)]
    dot_general x52 -> x32, matrix products: 121 us -> 57.4 us  [the longest x11 32.5 us: dot(): return jnp.dot(a, b, preferred_element_type=f32)]
    all_to_all x0 -> x9, starting transfers between devices: none -> 47.9 us  [exchange(): return lax.all_to_all(chunks, axes, 0, 0, tiled=True)]
  transfers between devices with their start and end apart: 22 -> 18, of which waited for: 18 -> 12; matrix products, arithmetic and copies ran while one was open for 3% -> 20% of each run, Pallas kernels for 0% -> 0%
where the time goes in v1:
time: 432 us; the launch traced here: 430 us
  waiting for transfers between devices  152 us (35%)
  matrix products  58.6 us (14%)
  blocking collectives  56.7 us (13%)
  local copies, waits for them, and re-layouts  56.5 us (13%)
  starting transfers between devices  55.4 us (13%)
  other arithmetic  33.8 us (8%)
  between operations  17.2 us (4%)
    all_to_all x9, waiting for transfers between devices, exchange(): return lax.all_to_all(chunks, axes, 0, 0, tiled=True)  98.1 us
    all_to_all x9, starting transfers between devices, exchange(): return lax.all_to_all(chunks, axes, 0, 0, tiled=True)  47.9 us
    all_to_all x2, blocking collectives, exchange(): return lax.all_to_all(chunks, axes, 0, 0, tiled=True)  46.5 us
    all_gather x2, waiting for transfers between devices, shards(): lax.all_gather(jnp.transpose(part, (1, 0, 2)).reshape(rows_here, 4 * half...  33.1 us
    dot_general x11, matrix products, dot(): return jnp.dot(a, b, preferred_element_type=f32)  32.5 us
    ppermute x7, waiting for transfers between devices, swap(): lax.ppermute(block, axis, [(i, i ^ mask) for i in range(lax.axis_size(axi...  20.5 us
    dot_general x5, matrix products, dot_nt(): lax.dot_general(a, b, (((1,), (1,)), ((), ())), preferred_element_type=f32)  17.7 us
    slice x1, local copies, waits for them, and re-layouts, encode_rows(): part = dot(inner, enc_down[layer]).astype(bf16)  11.3 us
  transfers between devices with their start and end apart: 18, of which 12 were waited for; matrix products, arithmetic and copies ran while one was open for 20% of the time, Pallas kernels for 0%

profile of v1, /device:TPU:2, one launch (start us, length us, event | category | flops | bytes accessed | tf_op | source)
XLA Modules:
  0.0 430.0 jit_solution(11106812364838349234)
XLA Ops:
  7.2 1.6 copy.196
  8.8 1.1 broadcast_select_fusion.2
  10.5 13.2 %collective-permute-done.6 = bf16[4,256,256]{1,2,0:T(8,128)(2,1)S(1)} collective-permute-done((bf16[4,256,256]{1,2,0:T(8,128)(2,1)S(1)}, bf16[4,256,256]{1,2,0:T(8,128)(2,1)S(1)}, u32[]{:S(2)}, u32[]{:S(2)}) %collective-permute-start.6) | collective-permute-done | bytes 524320 | tf_op jit(solution)/shard_map/ppermute | solution.py:32
  23.7 2.3 broadcast_select_fusion.1
  26.3 11.2 %fusion.224 = (bf16[1,1152,1076]{1,0,2:T(2,128)(2,1)}, bf16[1,1152,1076]{1,0,2:T(2,128)(2,1)}) fusion(bf16[2,1152,1076]{1,0,2:T(2,128)(2,1)} %param.27), kind=kLoop, calls=%fused_computation.388 | loop fusion | bytes 9916416 | tf_op jit(solution)/shard_map/slice | solution.py:84
  38.3 11.3 %fusion.225 = (bf16[1,1076,1152]{2,0,1:T(2,128)(2,1)}, bf16[1,1076,1152]{2,0,1:T(2,128)(2,1)}) fusion(bf16[2,1076,1152]{2,0,1:T(2,128)(2,1)} %param.28), kind=kLoop, calls=%fused_computation.389 | loop fusion | bytes 9916416 | tf_op jit(solution)/shard_map/slice | solution.py:85
  49.6 5.5 %fusion.22 = bf16[72,1152]{1,0:T(8,128)(2,1)S(1)} fusion(bf16[1,1076,1152]{2,0,1:T(2,128)(2,1)} %get-tuple-element.46, bf16[72,1152]{1,0:T(8,128)(2,1)S(1)} %convert_element_type.456, bf16[1,1152,1076]{1,0,2:T(2,128)(2,1)} %get-tuple-element.44), kind=kOutput, calls=%fused_computation.39 | convolution fusion | flops 357771168 | bytes 5289984 | tf_op jit(solution)/shard_map/dot_general | solution.py:20
  55.2 2.2 collective-permute-start.1
  57.4 1.2 collective-permute-start.2
  61.7 2.4 bitcast_select_fusion.1
  64.1 1.3 broadcast_compare_fusion
  67.2 7.4 %multiply_add_fusion = (s32[36]{0:T(128)S(1)}, s32[36]{0:T(128)S(1)}) fusion(s32[]{:T(128)} %bitcast.23, s32[]{:T(128)} %bitcast.22, s32[]{:T(128)} %bitcast.21, s32[]{:T(128)} %bitcast.20, s32[]{:T(128)} %bitcast.19, s32[]{:T(128)} %bitcast.18, s32[]{:T(128)} %bitcast.9, s32[]{:T(128)} %bitcast.8, s32[]{:T(128)} %bitcast.7, s32[]{:T(128)} %bitcast.6, ...), kind=kLoop, calls=%fused_computation.344 | loop fusion | flops 1404 | bytes 336 | tf_op jit(solution)/shard_map/add | solution.py:171
  74.7 1.4 convert_reduce_fusion.4
  76.3 5.4 %fusion.23 = bf16[72,1152]{1,0:T(8,128)(2,1)S(1)} fusion(bf16[1,1076,1152]{2,0,1:T(2,128)(2,1)} %get-tuple-element.45, bf16[1,1152,1076]{1,0,2:T(2,128)(2,1)} %get-tuple-element.43, bf16[72,1152]{1,0:T(8,128)(2,1)S(1)} %get-tuple-element.42, f32[72]{0:T(128)S(1)} %add_rsqrt_fusion.7, f32[72]{0:T(128)S(1)} %broadcast_multiply_fusion.5), kind=kOutput, calls=%fused_computation.40 | convolution fusion | flops 358102944 | bytes 5290560 | tf_op jit(solution)/shard_map/dot_general | solution.py:20
  82.2 2.1 collective-permute-start.4
  85.4 5.4 %collective-permute-done.4 = bf16[72,1152]{1,0:T(8,128)(2,1)S(1)} collective-permute-done((bf16[72,1152]{1,0:T(8,128)(2,1)S(1)}, bf16[72,1152]{1,0:T(8,128)(2,1)S(1)}, u32[]{:S(2)}, u32[]{:S(2)}) %collective-permute-start.4) | collective-permute-done | bytes 165920 | tf_op jit(solution)/shard_map/ppermute | solution.py:32
  90.8 1.8 collective-permute-done.5
  93.4 10.1 %all_gather.9 = bf16[72,4096]{1,0:T(8,128)(2,1)S(1)} all-gather(bf16[72,1024]{1,0:T(8,128)(2,1)S(1)} %convolution_convert_fusion.7), channel_id=1, replica_groups=mesh['segment'=2,'dp'=16,'vocab'=4] {'vocab'}, dimensions={1}, use_global_device_ids=true | all-gather | bytes 737280 | tf_op jit(solution)/shard_map/all_gather | solution.py:162
  103.5 1.2 fusion.11
  104.8 1.3 fusion.12
  107.1 6.4 %fusion.6 = f32[192,768]{1,0:T(8,128)} fusion(bf16[4096,1024]{0,1:T(8,128)(2,1)} %all-gather.3.cloned.1.call-done, bf16[192,4096]{1,0:T(8,128)(2,1)S(1)} %get-tuple-element.40, f32[192]{0:T(256)S(1)} %add_rsqrt_fusion.3), kind=kOutput, calls=%fused_computation.6 | convolution fusion | flops 1210318848 | bytes 8454912 | tf_op jit(solution)/shard_map/dot_general | solution.py:20
  113.4 1.4 reshape.685
  116.6 3.4 convolution_convert_fusion.1
  120.1 4.9 %all-to-all-start = ((bf16[8,24,4096]{2,1,0:T(8,128)(2,1)}), bf16[8,24,4096]{2,1,0:T(8,128)(2,1)S(1)}, u32[]{:S(2)}, u32[]{:S(2)}) async-start(bf16[8,24,4096]{2,1,0:T(8,128)(2,1)} %bitcast.37), calls=%async_computation | async-start | bytes 3145728 | tf_op jit(solution)/shard_map/all_to_all | solution.py:36
  124.9 20.2 %all-to-all-done = bf16[8,24,4096]{2,1,0:T(8,128)(2,1)S(1)} async-done(((bf16[8,24,4096]{2,1,0:T(8,128)(2,1)}), bf16[8,24,4096]{2,1,0:T(8,128)(2,1)S(1)}, u32[]{:S(2)}, u32[]{:S(2)}) %all-to-all-start) | async-done | bytes 1572896 | tf_op jit(solution)/shard_map/all_to_all | solution.py:36
  146.3 1.3 broadcast_in_dim.69
  147.6 4.9 %all-to-all-start.1 = ((bf16[8,24,4096]{2,1,0:T(8,128)(2,1)}), bf16[8,24,4096]{2,1,0:T(8,128)(2,1)S(1)}, u32[]{:S(2)}, u32[]{:S(2)}) async-start(bf16[8,24,4096]{2,1,0:T(8,128)(2,1)} %broadcast_in_dim.69), calls=%async_computation.1 | async-start | bytes 3145728 | tf_op jit(solution)/shard_map/all_to_all | solution.py:36
  153.9 33.1 %all-gather.5.cloned.1.call-done = bf16[4096,1024]{0,1:T(8,128)(2,1)} async-done(((bf16[256,1024]{0,1:T(8,128)(2,1)}), bf16[4096,1024]{0,1:T(8,128)(2,1)}) %all-gather.5.cloned.1.call-update) | async-done | bytes 8388624 | tf_op jit(solution)/shard_map/all_gather | solution.py:151
  187.0 6.2 %slice.338 = bf16[4096,768]{0,1:T(8,128)(2,1)} slice(bf16[4096,1024]{0,1:T(8,128)(2,1)} %all-gather.5.cloned.1.call-done), slice={[0:4096], [0:768]} | slice | bytes 12582912 | tf_op jit(solution)/shard_map/slice | solution.py:156
  194.0 4.3 %fusion.235 = f32[2,96,3,2,128]{4,1,3,2,0:T(8,128)S(1)} fusion(bf16[2,96,4096,1,1]{2,1,4,3,0:T(8,128)(2,1)S(1)} %bitcast.261, bf16[3,2,128,4096,1]{3,2,1,0,4:T(8,128)(2,1)} %bitcast.250), kind=kOutput, calls=%fused_computation.399 | convolution fusion | flops 1207959552 | bytes 8454144 | tf_op jit(solution)/shard_map/dot_general | solution.py:20
  200.2 2.6 convolution_convert_fusion.5
  202.8 4.8 %all-to-all-start.2 = ((bf16[8,8,512]{2,1,0:T(8,128)(2,1)}), bf16[8,8,512]{2,1,0:T(8,128)(2,1)S(1)}, u32[]{:S(2)}, u32[]{:S(2)}) async-start(bf16[8,8,512]{2,1,0:T(8,128)(2,1)} %bitcast.55), calls=%async_computation.2 | async-start | bytes 131072 | tf_op jit(solution)/shard_map/all_to_all | solution.py:36
  208.0 3.8 all-to-all-done.2
  211.8 1.1 broadcast_in_dim.70
  212.9 6.5 %all-to-all-start.3 = ((bf16[128,8,512]{2,1,0:T(8,128)(2,1)}), bf16[128,8,512]{2,1,0:T(8,128)(2,1)S(1)}, u32[]{:S(2)}, u32[]{:S(2)}) async-start(bf16[128,8,512]{2,1,0:T(8,128)(2,1)} %broadcast_in_dim.70), calls=%async_computation.3 | async-start | bytes 2097152 | tf_op jit(solution)/shard_map/all_to_all | solution.py:36
  224.1 13.1 %all-to-all-done.3 = bf16[128,8,512]{2,1,0:T(8,128)(2,1)S(1)} async-done(((bf16[128,8,512]{2,1,0:T(8,128)(2,1)}), bf16[128,8,512]{2,1,0:T(8,128)(2,1)S(1)}, u32[]{:S(2)}, u32[]{:S(2)}) %all-to-all-start.3) | async-done | bytes 1048608 | tf_op jit(solution)/shard_map/all_to_all | solution.py:36
  237.2 2.1 copy.204
  239.6 1.8 reshape.693
  241.6 3.3 exponential_reduce_fusion.1
  245.7 6.0 %all-to-all-start.4 = ((f32[128,4,128]{2,1,0:T(4,128)}), f32[128,4,128]{2,1,0:T(4,128)}, u32[]{:S(2)}, u32[]{:S(2)}) async-start(f32[128,4,128]{2,1,0:T(4,128)} %broadcast_in_dim.71), calls=%async_computation.4 | async-start | bytes 524288 | tf_op jit(solution)/shard_map/all_to_all | solution.py:36
  252.0 9.6 %all-to-all-done.4 = f32[128,4,128]{2,1,0:T(4,128)} async-done(((f32[128,4,128]{2,1,0:T(4,128)}), f32[128,4,128]{2,1,0:T(4,128)}, u32[]{:S(2)}, u32[]{:S(2)}) %all-to-all-start.4) | async-done | bytes 262176 | tf_op jit(solution)/shard_map/all_to_all | solution.py:36
  261.6 1.5 fusion.228
  263.8 2.2 convolution_convert_fusion.2
  266.1 22.5 %all_to_all.55 = bf16[128,8,512]{2,1,0:T(8,128)(2,1)S(1)} all-to-all(bf16[128,8,512]{2,1,0:T(8,128)(2,1)S(1)} %bitcast.251), channel_id=1, replica_groups=mesh['segment'=2,'dp'=16,'vocab'=4] {'segment','dp','vocab'}, dimensions={0} | all-to-all | bytes 2097152 | tf_op jit(solution)/shard_map/all_to_all | solution.py:36
  289.6 5.0 %all-to-all-start.6 = ((bf16[8,8,512]{2,1,0:T(8,128)(2,1)}), bf16[8,8,512]{2,1,0:T(8,128)(2,1)S(1)}, u32[]{:S(2)}, u32[]{:S(2)}) async-start(bf16[8,8,512]{2,1,0:T(8,128)(2,1)} %broadcast_in_dim.72), calls=%async_computation.6 | async-start | bytes 131072 | tf_op jit(solution)/shard_map/all_to_all | solution.py:36
  294.5 4.2 all-to-all-done.6
  300.7 2.2 fusion.57
  305.3 4.2 convolution_convert_fusion
  309.4 24.0 %all_to_all.56 = bf16[8,24,4096]{2,1,0:T(8,128)(2,1)S(1)} all-to-all(bf16[8,24,4096]{2,1,0:T(8,128)(2,1)S(1)} %bitcast.260), channel_id=1, replica_groups=mesh['segment'=2,'dp'=16,'vocab'=4] {'vocab','segment'}, dimensions={0} | all-to-all | bytes 3145728 | tf_op jit(solution)/shard_map/all_to_all | solution.py:36
  334.3 1.4 broadcast_in_dim.73
  335.7 4.9 %all-to-all-start.8 = ((bf16[8,24,4096]{2,1,0:T(8,128)(2,1)}), bf16[8,24,4096]{2,1,0:T(8,128)(2,1)S(1)}, u32[]{:S(2)}, u32[]{:S(2)}) async-start(bf16[8,24,4096]{2,1,0:T(8,128)(2,1)} %broadcast_in_dim.73), calls=%async_computation.8 | async-start | bytes 3145728 | tf_op jit(solution)/shard_map/all_to_all | solution.py:36
  341.5 19.3 %all-to-all-done.8 = bf16[8,24,4096]{2,1,0:T(8,128)(2,1)S(1)} async-done(((bf16[8,24,4096]{2,1,0:T(8,128)(2,1)}), bf16[8,24,4096]{2,1,0:T(8,128)(2,1)S(1)}, u32[]{:S(2)}, u32[]{:S(2)}) %all-to-all-start.8) | async-done | bytes 1572896 | tf_op jit(solution)/shard_map/all_to_all | solution.py:36
  360.8 3.1 fusion.38
  363.9 1.6 reshape.701
  365.5 1.1 fusion.43
  366.7 1.1 fusion.37
  367.8 1.2 fusion.47
  370.6 4.2 multiply_reduce_fusion.2
  376.0 4.9 %all-to-all-start.9 = ((bf16[8,80,512]{2,1,0:T(8,128)(2,1)}), bf16[8,80,512]{2,1,0:T(8,128)(2,1)S(1)}, u32[]{:S(2)}, u32[]{:S(2)}) async-start(bf16[8,80,512]{2,1,0:T(8,128)(2,1)} %pad_maximum_fusion.1), calls=%async_computation.9 | async-start | bytes 1310720 | tf_op jit(solution)/shard_map/all_to_all | solution.py:36
  381.8 9.4 %all-to-all-done.9 = bf16[8,80,512]{2,1,0:T(8,128)(2,1)S(1)} async-done(((bf16[8,80,512]{2,1,0:T(8,128)(2,1)}), bf16[8,80,512]{2,1,0:T(8,128)(2,1)S(1)}, u32[]{:S(2)}, u32[]{:S(2)}) %all-to-all-start.9) | async-done | bytes 655392 | tf_op jit(solution)/shard_map/all_to_all | solution.py:36
  393.2 1.2 reshape.704
  394.4 6.0 %all-to-all-start.10 = ((bf16[32,36,512]{2,1,0:T(8,128)(2,1)}), bf16[32,36,512]{2,1,0:T(8,128)(2,1)}, u32[]{:S(2)}, u32[]{:S(2)}) async-start(bf16[32,36,512]{2,1,0:T(8,128)(2,1)} %reshape.704), calls=%async_computation.10 | async-start | bytes 2621440 | tf_op jit(solution)/shard_map/all_to_all | solution.py:36
  401.1 18.5 %all-to-all-done.10 = bf16[32,36,512]{2,1,0:T(8,128)(2,1)} async-done(((bf16[32,36,512]{2,1,0:T(8,128)(2,1)}), bf16[32,36,512]{2,1,0:T(8,128)(2,1)}, u32[]{:S(2)}, u32[]{:S(2)}) %all-to-all-start.10) | async-done | bytes 1179680 | tf_op jit(solution)/shard_map/all_to_all | solution.py:36
  419.6 1.5 convert_reduce_fusion.2
  (282 shorter events, 37.1 us)
Async XLA Ops:
  7.2 85.6 %copy-start = (bf16[1152,1024]{1,0:T(8,128)(2,1)S(1)}, bf16[1152,1024]{1,0:T(8,128)(2,1)}, u32[]{:S(2)}) copy-start(bf16[1152,1024]{1,0:T(8,128)(2,1)} %param.29) | copy-start | bytes 7077892
  7.2 99.9 %all-gather.3.cloned.1.call-start = ((), (), s32[]{:S(2)}) async-start(), calls=%async_computation.11 | async-start | bytes 8912896 | tf_op jit(solution)/shard_map/all_gather | solution.py:151
  8.8 17.3 %copy-start.2 = (bf16[2,1,36,1152]{3,0,2,1:T(2,128)(2,1)S(1)}, bf16[2,1,36,1152]{3,0,2,1:T(2,128)(2,1)}, u32[]{:S(2)}) copy-start(bf16[2,1,36,1152]{3,0,2,1:T(2,128)(2,1)} %param.20) | copy-start | bytes 497668
  9.9 13.7 %collective-permute-start.6 = (bf16[4,256,256]{1,2,0:T(8,128)(2,1)S(1)}, bf16[4,256,256]{1,2,0:T(8,128)(2,1)S(1)}, u32[]{:S(2)}, u32[]{:S(2)}) collective-permute-start(bf16[4,256,256]{1,2,0:T(8,128)(2,1)S(1)} %broadcast_select_fusion.2), channel_id=1, source_target_pairs={{0,64},{64,0},{1,65},{65,1},{2,66},{66,2},{3,67},{67,3},{4,68},{68... | collective-permute-start | bytes 1572872 | tf_op jit(solution)/shard_map/ppermute | solution.py:32
  26.0 161.0 %all-gather.5.cloned.1.call-start = ((), (), s32[]{:S(2)}) async-start(), calls=%async_computation.12 | async-start | bytes 8912896 | tf_op jit(solution)/shard_map/all_gather | solution.py:151
  49.6 9.0 %copy-start.48 = (s32[2,1,4]{2,1,0:T(1,128)S(1)}, s32[2,1,4]{2,1,0:T(1,128)}, u32[]{:S(2)}) copy-start(s32[2,1,4]{2,1,0:T(1,128)} %param.25) | copy-start | bytes 100
  49.6 9.3 %copy-start.51 = (s32[2,1]{0,1:T(1,128)S(1)}, s32[2,1]{0,1:T(1,128)}, u32[]{:S(2)}) copy-start(s32[2,1]{0,1:T(1,128)} %param.23) | copy-start | bytes 28
  49.6 9.9 %copy-start.57 = (s32[2,1,6]{2,1,0:T(1,128)S(1)}, s32[2,1,6]{2,1,0:T(1,128)}, u32[]{:S(2)}) copy-start(s32[2,1,6]{2,1,0:T(1,128)} %param.24) | copy-start | bytes 148
  49.6 12.1 %copy-start.43 = (bf16[4096]{0:T(1024)(128)(2,1)S(1)}, bf16[4096]{0:T(1024)(128)(2,1)}, u32[]{:S(2)}) copy-start(bf16[4096]{0:T(1024)(128)(2,1)} %param.22) | copy-start | bytes 24580
  55.1 19.6 %copy-start.28 = (bf16[72,1152]{1,0:T(8,128)(2,1)}, bf16[72,1152]{1,0:T(8,128)(2,1)S(1)}, u32[]{:S(2)}) copy-start(bf16[72,1152]{1,0:T(8,128)(2,1)S(1)} %fusion.22) | copy-start | bytes 497668
  55.1 19.5 %collective-permute-start = (bf16[72,1152]{1,0:T(8,128)(2,1)S(1)}, bf16[72,1152]{1,0:T(8,128)(2,1)}, u32[]{:S(2)}, u32[]{:S(2)}) collective-permute-start(bf16[72,1152]{1,0:T(8,128)(2,1)S(1)} %fusion.22), channel_id=1, source_target_pairs={{0,1},{1,0},{2,3},{3,2},{4,5},{5,4},{6,7},{7,6},{8,9},{9,8},{10,11... | collective-permute-start | bytes 497672 | tf_op jit(solution)/shard_map/ppermute | solution.py:32
  55.2 19.5 %collective-permute-start.1 = (bf16[72,1152]{1,0:T(8,128)(2,1)S(1)}, bf16[72,1152]{1,0:T(8,128)(2,1)}, u32[]{:S(2)}, u32[]{:S(2)}) collective-permute-start(bf16[72,1152]{1,0:T(8,128)(2,1)S(1)} %fusion.22), channel_id=1, source_target_pairs={{0,2},{1,3},{2,0},{3,1},{4,6},{5,7},{6,4},{7,5},{8,10},{9,11},{10,... | collective-permute-start | bytes 497672 | tf_op jit(solution)/shard_map/ppermute | solution.py:32
  57.4 17.3 %collective-permute-start.2 = (bf16[72,1152]{1,0:T(8,128)(2,1)S(1)}, bf16[72,1152]{1,0:T(8,128)(2,1)}, u32[]{:S(2)}, u32[]{:S(2)}) collective-permute-start(bf16[72,1152]{1,0:T(8,128)(2,1)S(1)} %fusion.22), channel_id=1, source_target_pairs={{0,3},{1,2},{2,1},{3,0},{4,7},{5,6},{6,5},{7,4},{8,11},{9,10},{10,... | collective-permute-start | bytes 497672 | tf_op jit(solution)/shard_map/ppermute | solution.py:32
  58.8 94.3 %copy-start.46 = (f32[64]{0:T(128)}, f32[64]{0:T(128)S(1)}, u32[]{:S(2)}) copy-start(f32[64]{0:T(128)S(1)} %multiply_power_fusion) | copy-start | bytes 772
  58.9 17.2 %copy-start.49 = (f32[96]{0:T(128)}, f32[96]{0:T(128)S(1)}, u32[]{:S(2)}) copy-start(f32[96]{0:T(128)S(1)} %iota_convert_fusion) | copy-start | bytes 1156
  61.7 53.4 %copy-start.25 = (f32[96,64]{1,0:T(8,128)}, f32[96,64]{1,0:T(8,128)S(1)}, u32[]{:S(2)}) copy-start(f32[96,64]{1,0:T(8,128)S(1)} %get-tuple-element.85) | copy-start | bytes 73732
  65.4 38.2 %copy-start.55 = (pred[36]{0:T(512)(128)(4,1)}, pred[36]{0:T(512)(128)(4,1)S(1)}, u32[]{:S(2)}) copy-start(pred[36]{0:T(512)(128)(4,1)S(1)} %get-tuple-element.126) | copy-start | bytes 112
  65.4 39.4 %copy-start.62 = (pred[36]{0:T(512)(128)(4,1)}, pred[36]{0:T(512)(128)(4,1)S(1)}, u32[]{:S(2)}) copy-start(pred[36]{0:T(512)(128)(4,1)S(1)} %get-tuple-element.125) | copy-start | bytes 112
  74.6 28.9 %copy-start.53 = (s32[36]{0:T(128)}, s32[36]{0:T(128)S(1)}, u32[]{:S(2)}) copy-start(s32[36]{0:T(128)S(1)} %get-tuple-element.124) | copy-start | bytes 436
  74.7 30.1 %copy-start.59 = (s32[36]{0:T(128)}, s32[36]{0:T(128)S(1)}, u32[]{:S(2)}) copy-start(s32[36]{0:T(128)S(1)} %get-tuple-element.123) | copy-start | bytes 436
  81.7 3.7 collective-permute-start.3
  82.2 8.6 %collective-permute-start.4 = (bf16[72,1152]{1,0:T(8,128)(2,1)S(1)}, bf16[72,1152]{1,0:T(8,128)(2,1)S(1)}, u32[]{:S(2)}, u32[]{:S(2)}) collective-permute-start(bf16[72,1152]{1,0:T(8,128)(2,1)S(1)} %fusion.23), channel_id=1, source_target_pairs={{0,2},{1,3},{2,0},{3,1},{4,6},{5,7},{6,4},{7,5},{8,10},{9,11},{10,... | collective-permute-start | bytes 497672 | tf_op jit(solution)/shard_map/ppermute | solution.py:32
  84.4 8.3 %collective-permute-start.5 = (bf16[72,1152]{1,0:T(8,128)(2,1)S(1)}, bf16[72,1152]{1,0:T(8,128)(2,1)S(1)}, u32[]{:S(2)}, u32[]{:S(2)}) collective-permute-start(bf16[72,1152]{1,0:T(8,128)(2,1)S(1)} %fusion.23), channel_id=1, source_target_pairs={{0,3},{1,2},{2,1},{3,0},{4,7},{5,6},{6,5},{7,4},{8,11},{9,10},{10,... | collective-permute-start | bytes 497672 | tf_op jit(solution)/shard_map/ppermute | solution.py:32
  92.8 12.0 %copy-start.5 = (bf16[72,1152]{1,0:T(8,128)(2,1)}, bf16[72,1152]{1,0:T(8,128)(2,1)S(1)}, u32[]{:S(2)}) copy-start(bf16[72,1152]{1,0:T(8,128)(2,1)S(1)} %fusion.83) | copy-start | bytes 497668
  93.4 12.8 %copy-start.3 = (bf16[60,4096]{1,0:T(8,128)(2,1)S(1)}, bf16[60,4096]{1,0:T(8,128)(2,1)}, u32[]{:S(2)}) copy-start(bf16[60,4096]{1,0:T(8,128)(2,1)} %get-tuple-element.48) | copy-start | bytes 1474564
  107.0 6.4 %copy-start.4 = (bf16[192,4096]{1,0:T(8,128)(2,1)}, bf16[192,4096]{1,0:T(8,128)(2,1)S(1)}, u32[]{:S(2)}) copy-start(bf16[192,4096]{1,0:T(8,128)(2,1)S(1)} %get-tuple-element.40) | copy-start | bytes 4718596
  115.3 4.7 %copy-start.12 = (bf16[2,96,2,64]{3,1,2,0:T(8,128)(2,1)}, bf16[2,96,2,64]{3,1,2,0:T(8,128)(2,1)S(1)}, u32[]{:S(2)}) copy-start(bf16[2,96,2,64]{3,1,2,0:T(8,128)(2,1)S(1)} %get-tuple-element.71) | copy-start | bytes 147460
  115.3 4.7 %copy-start.14 = (bf16[2,96,2,64]{3,1,2,0:T(8,128)(2,1)}, bf16[2,96,2,64]{3,1,2,0:T(8,128)(2,1)S(1)}, u32[]{:S(2)}) copy-start(bf16[2,96,2,64]{3,1,2,0:T(8,128)(2,1)S(1)} %get-tuple-element.72) | copy-start | bytes 147460
  115.3 4.7 %copy-start.16 = (bf16[2,96,2,64]{3,1,2,0:T(8,128)(2,1)}, bf16[2,96,2,64]{3,1,2,0:T(8,128)(2,1)S(1)}, u32[]{:S(2)}) copy-start(bf16[2,96,2,64]{3,1,2,0:T(8,128)(2,1)S(1)} %get-tuple-element.59) | copy-start | bytes 147460
  115.3 4.7 %copy-start.17 = (bf16[2,96,2,64]{3,1,2,0:T(8,128)(2,1)}, bf16[2,96,2,64]{3,1,2,0:T(8,128)(2,1)S(1)}, u32[]{:S(2)}) copy-start(bf16[2,96,2,64]{3,1,2,0:T(8,128)(2,1)S(1)} %get-tuple-element.60) | copy-start | bytes 147460
  120.1 25.0 %all-to-all-start = ((bf16[8,24,4096]{2,1,0:T(8,128)(2,1)}), bf16[8,24,4096]{2,1,0:T(8,128)(2,1)S(1)}, u32[]{:S(2)}, u32[]{:S(2)}) async-start(bf16[8,24,4096]{2,1,0:T(8,128)(2,1)} %bitcast.37), calls=%async_computation | async-start | bytes 3145728 | tf_op jit(solution)/shard_map/all_to_all | solution.py:36
  147.6 45.6 %all-to-all-start.1 = ((bf16[8,24,4096]{2,1,0:T(8,128)(2,1)}), bf16[8,24,4096]{2,1,0:T(8,128)(2,1)S(1)}, u32[]{:S(2)}, u32[]{:S(2)}) async-start(bf16[8,24,4096]{2,1,0:T(8,128)(2,1)} %broadcast_in_dim.69), calls=%async_computation.1 | async-start | bytes 3145728 | tf_op jit(solution)/shard_map/all_to_all | solution.py:36
  153.1 54.6 %copy-start.35 = (bf16[8,192]{1,0:T(8,128)(2,1)}, bf16[8,192]{1,0:T(8,128)(2,1)S(1)}, u32[]{:S(2)}) copy-start(bf16[8,192]{1,0:T(8,128)(2,1)S(1)} %dynamic_update_slice.10) | copy-start | bytes 9220
  153.9 44.8 %copy-start.37 = (f32[2,4,64]{2,1,0:T(4,128)}, f32[2,4,64]{2,1,0:T(4,128)S(1)}, u32[]{:S(2)}) copy-start(f32[2,4,64]{2,1,0:T(4,128)S(1)} %get-tuple-element.83) | copy-start | bytes 6148
  198.5 9.4 %copy-start.20 = (bf16[2,96,2,64]{3,1,2,0:T(8,128)(2,1)}, bf16[2,96,2,64]{3,1,2,0:T(8,128)(2,1)S(1)}, u32[]{:S(2)}) copy-start(bf16[2,96,2,64]{3,1,2,0:T(8,128)(2,1)S(1)} %get-tuple-element.58) | copy-start | bytes 147460
  202.8 9.0 %all-to-all-start.2 = ((bf16[8,8,512]{2,1,0:T(8,128)(2,1)}), bf16[8,8,512]{2,1,0:T(8,128)(2,1)S(1)}, u32[]{:S(2)}, u32[]{:S(2)}) async-start(bf16[8,8,512]{2,1,0:T(8,128)(2,1)} %bitcast.55), calls=%async_computation.2 | async-start | bytes 131072 | tf_op jit(solution)/shard_map/all_to_all | solution.py:36
  212.9 24.3 %all-to-all-start.3 = ((bf16[128,8,512]{2,1,0:T(8,128)(2,1)}), bf16[128,8,512]{2,1,0:T(8,128)(2,1)S(1)}, u32[]{:S(2)}, u32[]{:S(2)}) async-start(bf16[128,8,512]{2,1,0:T(8,128)(2,1)} %broadcast_in_dim.70), calls=%async_computation.3 | async-start | bytes 2097152 | tf_op jit(solution)/shard_map/all_to_all | solution.py:36
  241.6 10.1 %copy-start.58 = (s32[2,16]{1,0:T(2,128)S(1)}, s32[2,16]{1,0:T(2,128)}, u32[]{:S(2)}) copy-start(s32[2,16]{1,0:T(2,128)} %param.26) | copy-start | bytes 388
  245.7 15.9 %all-to-all-start.4 = ((f32[128,4,128]{2,1,0:T(4,128)}), f32[128,4,128]{2,1,0:T(4,128)}, u32[]{:S(2)}, u32[]{:S(2)}) async-start(f32[128,4,128]{2,1,0:T(4,128)} %broadcast_in_dim.71), calls=%async_computation.4 | async-start | bytes 524288 | tf_op jit(solution)/shard_map/all_to_all | solution.py:36
  288.9 14.3 %copy-start.21 = (bf16[2,96,2,64]{3,1,2,0:T(8,128)(2,1)S(1)}, bf16[2,96,2,64]{3,1,2,0:T(8,128)(2,1)}, u32[]{:S(2)}) copy-start(bf16[2,96,2,64]{3,1,2,0:T(8,128)(2,1)} %copy-done.20) | copy-start | bytes 147460
  288.9 14.3 %copy-start.39 = (f32[2,2,4,96]{3,2,1,0:T(4,128)S(1)}, f32[2,2,4,96]{3,2,1,0:T(4,128)}, u32[]{:S(2)}) copy-start(f32[2,2,4,96]{3,2,1,0:T(4,128)} %get-tuple-element.120) | copy-start | bytes 18436
  288.9 14.3 %copy-start.41 = (f32[2,2,4]{2,1,0:T(2,128)S(1)}, f32[2,2,4]{2,1,0:T(2,128)}, u32[]{:S(2)}) copy-start(f32[2,2,4]{2,1,0:T(2,128)} %copy-done.40) | copy-start | bytes 196
  288.9 14.5 %copy-start.32 = (bf16[2,4,2,64]{3,1,2,0:T(4,128)(2,1)S(1)}, bf16[2,4,2,64]{3,1,2,0:T(4,128)(2,1)}, u32[]{:S(2)}) copy-start(bf16[2,4,2,64]{3,1,2,0:T(4,128)(2,1)} %copy-done.31) | copy-start | bytes 6148
  288.9 14.5 %copy-start.34 = (bf16[2,4,2,64]{3,1,2,0:T(4,128)(2,1)S(1)}, bf16[2,4,2,64]{3,1,2,0:T(4,128)(2,1)}, u32[]{:S(2)}) copy-start(bf16[2,4,2,64]{3,1,2,0:T(4,128)(2,1)} %copy-done.33) | copy-start | bytes 6148
  288.9 15.5 %copy-start.38 = (f32[2,4,64]{2,1,0:T(4,128)S(1)}, f32[2,4,64]{2,1,0:T(4,128)}, u32[]{:S(2)}) copy-start(f32[2,4,64]{2,1,0:T(4,128)} %copy-done.37) | copy-start | bytes 6148
  288.9 15.5 %copy-start.42 = (f32[2,4,64]{2,1,0:T(4,128)S(1)}, f32[2,4,64]{2,1,0:T(4,128)}, u32[]{:S(2)}) copy-start(f32[2,4,64]{2,1,0:T(4,128)} %get-tuple-element.81) | copy-start | bytes 6148
  288.9 15.6 %copy-start.36 = (bf16[8,192]{1,0:T(8,128)(2,1)S(1)}, bf16[8,192]{1,0:T(8,128)(2,1)}, u32[]{:S(2)}) copy-start(bf16[8,192]{1,0:T(8,128)(2,1)} %copy-done.35) | copy-start | bytes 9220
  289.6 15.2 %copy-start.27 = (f32[96,64]{1,0:T(8,128)S(1)}, f32[96,64]{1,0:T(8,128)}, u32[]{:S(2)}) copy-start(f32[96,64]{1,0:T(8,128)} %get-tuple-element.84) | copy-start | bytes 73732
  289.6 9.1 %all-to-all-start.6 = ((bf16[8,8,512]{2,1,0:T(8,128)(2,1)}), bf16[8,8,512]{2,1,0:T(8,128)(2,1)S(1)}, u32[]{:S(2)}, u32[]{:S(2)}) async-start(bf16[8,8,512]{2,1,0:T(8,128)(2,1)} %broadcast_in_dim.72), calls=%async_computation.6 | async-start | bytes 131072 | tf_op jit(solution)/shard_map/all_to_all | solution.py:36
  334.2 6.4 %copy-start.47 = (f32[64]{0:T(128)S(1)}, f32[64]{0:T(128)}, u32[]{:S(2)}) copy-start(f32[64]{0:T(128)} %copy-done.46) | copy-start | bytes 772
  334.3 6.3 %copy-start.50 = (f32[96]{0:T(128)S(1)}, f32[96]{0:T(128)}, u32[]{:S(2)}) copy-start(f32[96]{0:T(128)} %copy-done.49) | copy-start | bytes 1156
  334.3 7.1 %copy-start.9 = (bf16[36,4096]{1,0:T(8,128)(2,1)S(1)}, bf16[36,4096]{1,0:T(8,128)(2,1)}, u32[]{:S(2)}) copy-start(bf16[36,4096]{1,0:T(8,128)(2,1)} %copy-done.8) | copy-start | bytes 884740
  334.3 7.1 %copy-start.11 = (bf16[36,4096]{1,0:T(8,128)(2,1)S(1)}, bf16[36,4096]{1,0:T(8,128)(2,1)}, u32[]{:S(2)}) copy-start(bf16[36,4096]{1,0:T(8,128)(2,1)} %copy-done.10) | copy-start | bytes 884740
  335.7 25.1 %all-to-all-start.8 = ((bf16[8,24,4096]{2,1,0:T(8,128)(2,1)}), bf16[8,24,4096]{2,1,0:T(8,128)(2,1)S(1)}, u32[]{:S(2)}, u32[]{:S(2)}) async-start(bf16[8,24,4096]{2,1,0:T(8,128)(2,1)} %broadcast_in_dim.73), calls=%async_computation.8 | async-start | bytes 3145728 | tf_op jit(solution)/shard_map/all_to_all | solution.py:36
  360.8 5.9 %copy-start.45 = (f32[2,2,96]{2,1,0:T(2,128)S(1)}, f32[2,2,96]{2,1,0:T(2,128)}, u32[]{:S(2)}) copy-start(f32[2,2,96]{2,1,0:T(2,128)} %copy-done.44) | copy-start | bytes 4612
  363.9 5.1 %copy-start.13 = (bf16[2,96,2,64]{3,1,2,0:T(8,128)(2,1)S(1)}, bf16[2,96,2,64]{3,1,2,0:T(8,128)(2,1)}, u32[]{:S(2)}) copy-start(bf16[2,96,2,64]{3,1,2,0:T(8,128)(2,1)} %copy-done.12) | copy-start | bytes 147460
  376.0 16.3 %copy-start.54 = (s32[36]{0:T(128)S(1)}, s32[36]{0:T(128)}, u32[]{:S(2)}) copy-start(s32[36]{0:T(128)} %copy-done.53) | copy-start | bytes 436
  376.0 16.3 %copy-start.56 = (pred[36]{0:T(512)(128)(4,1)S(1)}, pred[36]{0:T(512)(128)(4,1)}, u32[]{:S(2)}) copy-start(pred[36]{0:T(512)(128)(4,1)} %copy-done.55) | copy-start | bytes 112
  376.0 16.5 %copy-start.60 = (s32[36]{0:T(128)S(1)}, s32[36]{0:T(128)}, u32[]{:S(2)}) copy-start(s32[36]{0:T(128)} %copy-done.59) | copy-start | bytes 436
  376.0 16.5 %copy-start.63 = (pred[36]{0:T(512)(128)(4,1)S(1)}, pred[36]{0:T(512)(128)(4,1)}, u32[]{:S(2)}) copy-start(pred[36]{0:T(512)(128)(4,1)} %copy-done.62) | copy-start | bytes 112
  376.0 15.2 %all-to-all-start.9 = ((bf16[8,80,512]{2,1,0:T(8,128)(2,1)}), bf16[8,80,512]{2,1,0:T(8,128)(2,1)S(1)}, u32[]{:S(2)}, u32[]{:S(2)}) async-start(bf16[8,80,512]{2,1,0:T(8,128)(2,1)} %pad_maximum_fusion.1), calls=%async_computation.9 | async-start | bytes 1310720 | tf_op jit(solution)/shard_map/all_to_all | solution.py:36
  381.8 10.9 %copy-start.6 = (bf16[72,1152]{1,0:T(8,128)(2,1)S(1)}, bf16[72,1152]{1,0:T(8,128)(2,1)}, u32[]{:S(2)}) copy-start(bf16[72,1152]{1,0:T(8,128)(2,1)} %copy-done.5) | copy-start | bytes 497668
  393.2 28.8 %copy-start.1 = (bf16[1152,1024]{1,0:T(8,128)(2,1)S(1)}, bf16[1152,1024]{1,0:T(8,128)(2,1)}, u32[]{:S(2)}) copy-start(bf16[1152,1024]{1,0:T(8,128)(2,1)} %param.29) | copy-start | bytes 7077892
  394.4 25.2 %all-to-all-start.10 = ((bf16[32,36,512]{2,1,0:T(8,128)(2,1)}), bf16[32,36,512]{2,1,0:T(8,128)(2,1)}, u32[]{:S(2)}, u32[]{:S(2)}) async-start(bf16[32,36,512]{2,1,0:T(8,128)(2,1)} %reshape.704), calls=%async_computation.10 | async-start | bytes 2621440 | tf_op jit(solution)/shard_map/all_to_all | solution.py:36
  (18 other events, 57.8 us)
Sparse Core Ops, SparseCore 0:
  26.2 80.8 all-gather.2
  109.2 77.7 all-gather.4

commit v2 on v1

v2 whole, which is shorter than its diff:
```python
import functools

import jax
import jax.numpy as jnp
from jax import lax
from jax.experimental import pallas as pl
from jax.experimental.pallas import tpu as pltpu
from jax.sharding import PartitionSpec as P

HD = 128
MASKED = 4
RATIOS = 8

epsilon = 1e-06
rope_base = 500000.0

LINE = ("vocab", "segment")
ALL = ("segment", "dp", "vocab")
f32 = jnp.float32
bf16 = jnp.bfloat16


def dot(a, b):
    return jnp.dot(a, b, preferred_element_type=f32)


def dot_nt(a, b):
    return lax.dot_general(a, b, (((1,), (1,)), ((), ())), preferred_element_type=f32)


def dot_tn(a, b):
    return lax.dot_general(a, b, (((0,), (0,)), ((), ())), preferred_element_type=f32)


def swap(block, axis, mask):
    return lax.ppermute(block, axis, [(i, i ^ mask) for i in range(lax.axis_size(axis))])


def exchange(chunks, axes):
    return lax.all_to_all(chunks, axes, 0, 0, tiled=True)


def spread(block, axes):
    size = lax.axis_size(axes)
    return exchange(jnp.broadcast_to(block[None], (size,) + block.shape), axes)


def inverse_rms(values_in):
    return lax.rsqrt(jnp.mean(values_in * values_in, axis=-1, keepdims=True) + epsilon)


def norm_rows(values_in):
    return values_in * inverse_rms(values_in)


def layer_norm(values_in):
    centred = values_in - jnp.mean(values_in, axis=-1, keepdims=True)
    return centred * lax.rsqrt(jnp.mean(centred * centred, axis=-1, keepdims=True) + epsilon)


def norm_back(values_in, cotangent):
    factor = inverse_rms(values_in)
    return factor * cotangent - values_in * factor**3 * jnp.mean(
        cotangent * values_in, axis=-1, keepdims=True
    )


SIDE = ("dp", "vocab")
TOKENS = ("segment", "vocab")


def in_vmem():
    return pl.BlockSpec(memory_space=pltpu.VMEM)


def call(body, name, outs, *args, smem=0):
    specs = [
        pl.BlockSpec(memory_space=pltpu.SMEM) if i < smem else in_vmem() for i in range(len(args))
    ]
    return pl.pallas_call(
        body,
        name=name,
        out_shape=[jax.ShapeDtypeStruct(shape, kind) for shape, kind in outs],
        in_specs=specs,
        out_specs=[in_vmem() for _ in outs],
        compiler_params=pltpu.CompilerParams(vmem_limit_bytes=56 << 20),
    )(*args)


def side_shift(block, step, first):
    sizes = (lax.axis_size("dp"), lax.axis_size("vocab"))
    edge = 4
    route = []
    for dp in range(sizes[0]):
        z, y = divmod(dp, edge)
        for v in range(sizes[1]):
            if (v % 2 == 0) == first:
                to = z * edge + (y + step) % edge
            else:
                to = ((z + step) % edge) * edge + y
            route.append((dp * sizes[1] + v, to * sizes[1] + v))
    return lax.ppermute(block, SIDE, route)


def line_move(block, lo, hi):
    count = lax.axis_size("vocab")
    route = [
        (s * count + v, (s ^ lo) * count + (v ^ (2 * hi)))
        for s in range(lax.axis_size("segment"))
        for v in range(count)
    ]
    return lax.ppermute(block, TOKENS, route)


def sum_rows(partial, core, chip):
    rows, width = partial.shape
    halves = partial.reshape(2, rows // 2, width)
    other = lax.dynamic_index_in_dim(halves, 1 - core, 0, False)
    mine = lax.dynamic_index_in_dim(halves, core, 0, False)
    both = (mine.astype(f32) + swap(other, "vocab", 1).astype(f32)).astype(bf16)
    both = both.reshape(4, rows // 8, width)

    def piece(mask):
        return lax.dynamic_index_in_dim(both, chip ^ mask, 0, False)

    moved = [line_move(piece(m), m & 1, m >> 1) for m in (1, 2, 3)]
    return (piece(0).astype(f32) + moved[0].astype(f32)) + (
        moved[1].astype(f32) + moved[2].astype(f32)
    )


def spread_rows(block, core, chip):
    rows, width = block.shape
    pieces = [block] + [line_move(block, m & 1, m >> 1) for m in (1, 2, 3)]
    half = jnp.zeros((4, rows, width), block.dtype)
    for mask in range(4):
        half = lax.dynamic_update_slice(half, pieces[mask][None], (chip ^ mask, 0, 0))
    other = swap(half, "vocab", 1)
    whole = jnp.zeros((2, 4, rows, width), block.dtype)
    whole = lax.dynamic_update_slice(whole, half[None], (core, 0, 0, 0))
    whole = lax.dynamic_update_slice(whole, other[None], (1 - core, 0, 0, 0))
    return whole.reshape(8 * rows, width)


def prepare(counts, order, masks, up, down, up_out, down_out, placing_out, pick_out, masked_out):
    up_out[...] = up[...].reshape(up_out.shape)
    down_out[...] = down[...].reshape(down_out.shape)
    micro, slots, _ = placing_out.shape
    images = order.shape[1]
    each = slots // images
    cell = lax.broadcasted_iota(jnp.int32, (slots, slots), 0)
    slot = lax.broadcasted_iota(jnp.int32, (slots, slots), 1)
    tokens = pick_out.shape[1]
    seq_len = tokens // micro
    row = lax.broadcasted_iota(jnp.int32, pick_out.shape, 0)
    column = lax.broadcasted_iota(jnp.int32, pick_out.shape, 1)
    token = lax.broadcasted_iota(jnp.int32, masked_out.shape, 0)
    pick = jnp.zeros(pick_out.shape, f32)
    masked = jnp.zeros(masked_out.shape, f32)
    for m in range(micro):
        hit = jnp.zeros((slots, slots), f32)
        for i in range(images):
            within = slot - i * each
            inside = (within >= 0) & (within < each) & (cell == order[m, i] * each + within)
            live = jnp.where(i < counts[m, 0], 1.0, 0.0)
            hit = jnp.where(inside, live, hit)
        placing_out[m] = hit.astype(bf16)
        for p in range(MASKED):
            where = m * seq_len + masks[m, p]
            pick = jnp.where((row == m * MASKED + p) & (column == where), 1.0, pick)
            masked = jnp.where(token == where, 1.0, masked)
    pick_out[...] = pick.astype(bf16)
    masked_out[...] = masked


def add_parts(x, parts):
    total = parts[0][...].astype(f32) + parts[1][...].astype(f32)
    total = total + (parts[2][...].astype(f32) + parts[3][...].astype(f32))
    return (x[...].astype(f32) + total).astype(bf16)


def mlp(layer, layers, current, up, down):
    normed = layer_norm(current.astype(f32)).astype(bf16)
    inner = dot_nt(normed, up[...])
    mine = lax.broadcasted_iota(jnp.int32, inner.shape, 1) % layers == layer
    inner = jnp.where(mine, jax.nn.gelu(inner, approximate=True), 0.0).astype(bf16)
    return dot(inner, down[...]).astype(bf16)


def encode_first(layers, x, up, down, part):
    part[...] = mlp(0, layers, x[...], up, down)


def encode_next(layer, layers, x, p0, p1, p2, p3, up, down, part, current):
    now = add_parts(x, (p0, p1, p2, p3))
    current[...] = now
    part[...] = mlp(layer, layers, now, up, down)


def encode_last(x, p0, p1, p2, p3, projector, current, columns):
    now = add_parts(x, (p0, p1, p2, p3))
    current[...] = now
    columns[...] = dot(now, projector[...]).astype(bf16)


def turn(values, cosine, sine):
    return values * cosine + pltpu.roll(values, HD // 2, 1) * sine


def softmax(scores):
    powers = jnp.exp(scores - jnp.max(scores, axis=-1, keepdims=True))
    return powers / jnp.sum(powers, axis=-1, keepdims=True)


def project_heads(hidden, w, cosine, sine, q_out, k_out, v_out):
    half = q_out.shape[1]
    normed = norm_rows(hidden.astype(f32)).astype(bf16)
    all_heads = dot(normed, w[:, : 3 * half])
    tokens = hidden.shape[0]
    seq_len = cosine.shape[0]
    for m in range(tokens // seq_len):
        rows = slice(m * seq_len, (m + 1) * seq_len)
        for h in range(half // HD):
            cols = slice(h * HD, (h + 1) * HD)
            q = all_heads[rows, h * HD : (h + 1) * HD]
            k = all_heads[rows, half + h * HD : half + (h + 1) * HD]
            q_out[rows, cols] = turn(q, cosine[...], sine[...]).astype(bf16)
            k_out[rows, cols] = turn(k, cosine[...], sine[...]).astype(bf16)
    v_out[...] = all_heads[:, 2 * half :].astype(bf16)


def attend(q, k, v):
    probs = softmax(dot_nt(q, k) * HD ** (-0.5))
    return dot(probs.astype(bf16), v).astype(bf16)


def attend_back(q, k, v, d_mixed):
    probs = softmax(dot_nt(q, k) * HD ** (-0.5))
    d_probs = dot_nt(d_mixed, v).astype(bf16).astype(f32)
    d_scores = probs * (d_probs - jnp.sum(probs * d_probs, axis=-1, keepdims=True))
    return (d_scores * HD ** (-0.5)).astype(bf16), probs.astype(bf16)


def first_section(
    images, text, mask_row, placing, masked, w, cosine, sine, hidden, q, k, v, partial, mixed
):
    micro, slots, _ = placing.shape
    seq_len = cosine.shape[0]
    tokens, width = hidden.shape
    blocks = images.shape[0] // micro
    part = width // blocks
    half = q.shape[1]
    for m in range(micro):
        rows = slice(m * seq_len, (m + 1) * seq_len)
        hidden[rows, :] = jnp.where(masked[rows, :] > 0.0, mask_row[...], text[m])
        place = placing[m]
        filled = jnp.sum(place.astype(f32), axis=1, keepdims=True) > 0.0
        for b in range(blocks):
            placed = dot(place, images[m * blocks + b]).astype(bf16)
            cols = slice(b * part, (b + 1) * part)
            hidden[m * seq_len : m * seq_len + slots, cols] = jnp.where(
                filled, placed, text[m, :slots, cols]
            )
    project_heads(hidden[...], w, cosine, sine, q, k, v)
    for m in range(micro):
        rows = slice(m * seq_len, (m + 1) * seq_len)
        for h in range(half // HD):
            cols = slice(h * HD, (h + 1) * HD)
            mixed[rows, cols] = attend(q[rows, cols], k[rows, cols], v[rows, cols])
    partial[...] = dot_nt(mixed[...], w[:, 3 * half :]).astype(bf16)


def last_section(hidden, pick, w, cosine, sine, q, k, v, partial, picked, q_all, mixed):
    half = k.shape[1]
    seq_len = cosine.shape[0]
    project_heads(hidden[...], w, cosine, sine, q_all, k, v)
    for m in range(hidden.shape[0] // seq_len):
        rows = slice(m * seq_len, (m + 1) * seq_len)
        mine = slice(m * MASKED, (m + 1) * MASKED)
        q_mine = dot(pick[...], q_all[...]).astype(bf16)[mine]
        q[mine, :] = q_mine
        for h in range(half // HD):
            cols = slice(h * HD, (h + 1) * HD)
            mixed[mine, cols] = attend(q_mine[:, cols], k[rows, cols], v[rows, cols])
    partial[...] = dot_nt(mixed[...], w[:, 3 * half :]).astype(bf16)
    picked[...] = dot(pick[...], hidden[...])


def last_section_back(grad, pick, q, k, v, w, cosine, sine, partial, d_all):
    half = k.shape[1]
    seq_len = cosine.shape[0]
    d_mixed = dot(grad[...], w[:, 3 * half :]).astype(bf16)
    for m in range(k.shape[0] // seq_len):
        rows = slice(m * seq_len, (m + 1) * seq_len)
        mine = slice(m * MASKED, (m + 1) * MASKED)
        spot = pick[mine, rows]
        for h in range(half // HD):
            cols = slice(h * HD, (h + 1) * HD)
            q_h, k_h, d_h = q[mine, cols], k[rows, cols], d_mixed[mine, cols]
            d_scores, probs = attend_back(q_h, k_h, v[rows, cols], d_h)
            d_q = dot_tn(spot, dot(d_scores, k_h).astype(bf16))
            d_k = dot_tn(d_scores, q_h).astype(bf16).astype(f32)
            d_v = dot_tn(probs, d_h)
            for part, d in enumerate(
                (turn(d_q, cosine[...], -sine[...]), turn(d_k, cosine[...], -sine[...]), d_v)
            ):
                at = part * half + h * HD
                d_all[rows, at : at + HD] = d.astype(bf16)
    partial[...] = dot_nt(d_all[...], w[:, : 3 * half]).astype(bf16)


def first_section_back(
    slots, grad, hidden, q, k, v, w, cosine, sine, partial, along, d_all
):
    half = k.shape[1]
    seq_len = cosine.shape[0]
    d_mixed = dot(grad[...], w[:, 3 * half :]).astype(bf16)
    micro = k.shape[0] // seq_len
    cos_top, sin_top = cosine[:slots, :], -sine[:slots, :]
    for m in range(micro):
        rows = slice(m * seq_len, (m + 1) * seq_len)
        top = slice(m * slots, (m + 1) * slots)
        for h in range(half // HD):
            cols = slice(h * HD, (h + 1) * HD)
            q_h, k_h, d_h = q[rows, cols], k[rows, cols], d_mixed[rows, cols]
            d_scores, probs = attend_back(q_h, k_h, v[rows, cols], d_h)
            d_q = dot(d_scores, k_h)[:slots].astype(bf16).astype(f32)
            d_k = dot_tn(d_scores, q_h)[:slots].astype(bf16).astype(f32)
            d_v = dot_tn(probs, d_h)[:slots]
            for part, d in enumerate(
                (turn(d_q, cos_top, sin_top), turn(d_k, cos_top, sin_top), d_v)
            ):
                at = part * half + h * HD
                d_all[top, at : at + HD] = d
    rounded = dot_nt(d_all[...].astype(bf16), w[:, : 3 * half]).astype(bf16)
    partial[...] = rounded
    for m in range(micro):
        top = slice(m * slots, (m + 1) * slots)
        own = hidden[m * seq_len : m * seq_len + slots, :].astype(f32)
        along[top, :] = jnp.mean(rounded[top, :].astype(f32) * own, axis=1, keepdims=True)


def collect(targets, near, ahead, far_low, far_high, behind, out, sems):
    rows = near.shape[1]
    copies = []
    sources = [near.at[i] for i in range(4)] + [ahead.at[i] for i in range(4)]
    sources += [far_low.at[0], far_low.at[1], far_high.at[0], far_high.at[1]]
    sources += [behind.at[i] for i in range(4)]
    for i, source in enumerate(sources):
        start = pl.multiple_of(targets[i] * rows, rows)
        copies.append(pltpu.make_async_copy(source, out.at[pl.ds(start, rows)], sems.at[i]))
    for copy in copies:
        copy.start()
    for copy in copies:
        copy.wait()


def collected(targets, near, ahead, far_low, far_high, behind):
    rows, cols = near.shape[1:]
    return pl.pallas_call(
        collect,
        name="collect",
        out_shape=jax.ShapeDtypeStruct((16 * rows, cols), near.dtype),
        in_specs=[pl.BlockSpec(memory_space=pltpu.SMEM)]
        + [pl.BlockSpec(memory_space=pl.ANY)] * 5,
        out_specs=pl.BlockSpec(memory_space=pl.ANY),
        scratch_shapes=[pltpu.SemaphoreType.DMA((16,))],
    )(targets, near, ahead, far_low, far_high, behind)


def gather_weights(sections, dp_index, core):
    both = jnp.stack(sections)
    behind = side_shift(both, 1, True)
    ahead = side_shift(both, -1, True)
    far = [side_shift(behind[0], 1, True), side_shift(ahead[1], -1, True)]
    z, y = dp_index // 4, dp_index % 4
    step = jnp.arange(4, dtype=jnp.int32)
    outer = jnp.where(core == 0, z, y)
    inner = jnp.where(core == 0, y, z)
    outer = ((outer + step) % 4)[:, None]
    inner = ((inner + step) % 4)[None, :]
    targets = jnp.where(core == 0, outer * 4 + inner, inner * 4 + outer).reshape(-1)
    whole = []
    for s in range(2):
        near = jnp.stack([both[s], ahead[s], far[s], behind[s]])
        from_behind = side_shift(near, 1, False)
        from_ahead = side_shift(near, -1, False)
        low = side_shift(from_behind[:2], 1, False)
        high = side_shift(from_ahead[2:], -1, False)
        whole.append(collected(targets, near, from_ahead, low, high, from_behind))
    return whole


def shards(
    patches,
    text_embed,
    mask_embed,
    image_counts,
    image_order,
    masked_positions,
    ratio_index,
    enc_up,
    enc_down,
    projector,
    lang_qkv,
    lang_out,
    head_weight,
    teacher_logits,
):
    segment = lax.axis_index("segment")
    dp_index = lax.axis_index("dp")
    place = lax.axis_index("vocab") * 2 + segment
    core = lax.axis_index("vocab") % 2
    chip = (lax.axis_index("vocab") // 2) * 2 + segment
    line = lax.axis_size(LINE)
    dp_size = lax.axis_size("dp")
    micro = text_embed.shape[0]
    seq_len, width = text_embed.shape[2:]
    slots = patches.shape[2]
    depth = patches.shape[3]

    shard = jnp.concatenate(
        [lang_qkv[0], jnp.transpose(lang_out[0])[None]], axis=0
    )
    half = shard.shape[2] // 2
    rows_here = shard.shape[1]
    low, high = shard[:, :, :half], shard[:, :, half:]
    keep = jnp.where(segment == 0, low, high)
    give = jnp.where(segment == 0, high, low)
    got = swap(give, "segment", 1)
    sections = (
        jnp.where(segment == 0, keep, got),
        jnp.where(segment == 0, got, keep),
    )
    w_first, w_last = gather_weights(
        [jnp.transpose(part, (1, 0, 2)).reshape(rows_here, 4 * half) for part in sections],
        dp_index,
        core,
    )

    layers, _, hidden_units = enc_up.shape
    tokens = micro * seq_len
    masked_rows = micro * MASKED
    up, down, placing, pick_all, masked = call(
        prepare,
        "prepare",
        [
            ((layers * hidden_units, depth), bf16),
            ((layers * hidden_units, depth), bf16),
            ((micro, slots, slots), bf16),
            ((masked_rows, tokens), bf16),
            ((tokens, 1), f32),
        ],
        image_counts,
        image_order[:, 0],
        masked_positions[:, 0],
        jnp.transpose(enc_up, (2, 0, 1)),
        jnp.transpose(enc_down, (1, 0, 2)),
        smem=3,
    )

    def parts_of(part):
        return [part] + [swap(part, "vocab", mask) for mask in (1, 2, 3)]

    small = ((slots, depth), bf16)
    current = lax.dynamic_index_in_dim(patches[:, 0], segment, 0, False)
    (part,) = call(
        functools.partial(encode_first, layers), "encode_first", [small], current, up, down
    )
    for layer in range(1, layers):
        part, current = call(
            functools.partial(encode_next, layer, layers),
            "encode_next",
            [small, small],
            current,
            *parts_of(part),
            up,
            down,
        )
    encoded_own, image_cols = call(
        encode_last,
        "encode_last",
        [small, ((slots, projector.shape[1]), bf16)],
        current,
        *parts_of(part),
        projector,
    )
    images = spread(image_cols, TOKENS).reshape(line, slots, projector.shape[1])
    encoded_other = swap(encoded_own, "segment", 1)
    encoded = jnp.concatenate(
        [
            jnp.where(segment == 0, encoded_own, encoded_other),
            jnp.where(segment == 0, encoded_other, encoded_own),
        ],
        axis=0,
    )

    angles = jnp.arange(seq_len, dtype=f32)[:, None] * (
        rope_base ** (-2.0 * jnp.arange(HD // 2, dtype=f32) / HD)
    )
    cosine = jnp.concatenate([jnp.cos(angles), jnp.cos(angles)], axis=1)
    sine = jnp.concatenate([-jnp.sin(angles), jnp.sin(angles)], axis=1)
    chunk_rows = tokens // line
    row_start = (core * 4 + chip) * chunk_rows
    whole = ((tokens, width), bf16)
    heads = ((tokens, half), bf16)

    def own_rows(array):
        return lax.dynamic_slice_in_dim(array, row_start, chunk_rows, 0)

    hidden0, q0, k0, v0, partial, _ = call(
        first_section,
        "first_section",
        [whole, heads, heads, heads, whole, heads],
        images,
        text_embed[:, 0],
        mask_embed[None, :],
        placing,
        masked,
        w_first,
        cosine,
        sine,
    )
    mine = (own_rows(hidden0).astype(f32) + sum_rows(partial, core, chip)).astype(bf16)
    hidden1 = spread_rows(mine, core, chip)

    few_heads = ((masked_rows, half), bf16)
    q1, k1, v1, partial, picked, _, _ = call(
        last_section,
        "last_section",
        [
            few_heads,
            heads,
            heads,
            ((masked_rows, width), bf16),
            ((masked_rows, width), f32),
            heads,
            few_heads,
        ],
        hidden1,
        pick_all,
        w_last,
        cosine,
        sine,
    )
    cols = width // line
    parts = exchange(
        jnp.transpose(partial.reshape(masked_rows, line, cols), (1, 0, 2)), LINE
    )
    picked = lax.dynamic_slice_in_dim(picked, place * cols, cols, 1)
    last = (picked + jnp.sum(parts.astype(f32), axis=0)).astype(bf16)

    all_rows = spread(last, ALL).reshape(2, dp_size, 4, masked_rows, cols)
    all_rows = jnp.transpose(all_rows, (1, 3, 2, 0, 4)).reshape(dp_size * masked_rows, width)
    row_count = all_rows.shape[0]
    final = norm_rows(all_rows.astype(f32)).astype(bf16)
    logits = dot_nt(final, head_weight)

    teacher = (
        jnp.transpose(teacher_logits.reshape(micro, dp_size, MASKED, -1), (1, 0, 2, 3))
        .reshape(row_count, -1)
        .astype(f32)
    )
    top = jnp.max(teacher, axis=1)
    powers = jnp.exp(teacher - top[:, None])
    stats = jnp.stack(
        [
            jnp.sum(jnp.exp(logits), axis=1),
            top,
            jnp.sum(powers, axis=1),
            jnp.sum(powers * (teacher - logits), axis=1),
        ]
    )
    stats = spread(stats, ALL).reshape(-1, 4, row_count)
    sum_student = jnp.sum(stats[:, 0], axis=0)
    top_all = jnp.max(stats[:, 1], axis=0)
    scale = jnp.exp(stats[:, 1] - top_all[None])
    sum_teacher = jnp.sum(stats[:, 2] * scale, axis=0)
    cross = jnp.sum(stats[:, 3] * scale, axis=0)
    norm_student = jnp.log(sum_student)
    norm_teacher = top_all + jnp.log(sum_teacher)
    divergence = cross / sum_teacher - norm_teacher + norm_student
    ratio = RATIOS / ratio_index.astype(f32)
    row_weights = jnp.repeat(jnp.transpose(ratio), MASKED, axis=1).reshape(-1)
    total = micro * dp_size
    loss = jnp.sum(row_weights * divergence) / total
    d_logits = (
        (row_weights / total)[:, None]
        * (jnp.exp(logits - norm_student[:, None]) - jnp.exp(teacher - norm_teacher[:, None]))
    ).astype(bf16)
    d_final = dot(d_logits, head_weight).astype(bf16)
    d_final = jnp.transpose(
        d_final.reshape(dp_size, masked_rows, 4, 2, cols), (3, 0, 2, 1, 4)
    ).reshape(-1, masked_rows, cols)
    d_own = jnp.sum(exchange(d_final, ALL).astype(f32), axis=0).astype(bf16)
    d_own = jnp.transpose(spread(d_own, LINE).reshape(line, masked_rows, cols), (1, 0, 2)).reshape(
        masked_rows, width
    )
    rows = lax.dynamic_slice_in_dim(all_rows, dp_index * masked_rows, masked_rows, 0)
    grad_rows = norm_back(rows.astype(f32), d_own.astype(f32)).astype(bf16)

    partial, _ = call(
        last_section_back,
        "last_section_back",
        [whole, ((tokens, 3 * half), bf16)],
        grad_rows,
        pick_all,
        q1,
        k1,
        v1,
        w_last,
        cosine,
        sine,
    )
    d_normed = sum_rows(partial, core, chip)
    own_pick = lax.dynamic_slice_in_dim(pick_all, row_start, chunk_rows, 1)
    grad_own = dot_tn(own_pick, grad_rows)
    grad_own = (grad_own + norm_back(own_rows(hidden1).astype(f32), d_normed)).astype(bf16)
    grad = spread_rows(grad_own, core, chip)

    cells = micro * slots
    partial, along, _ = call(
        functools.partial(first_section_back, slots),
        "first_section_back",
        [((cells, width), bf16), ((cells, 1), f32), ((cells, 3 * half), f32)],
        grad,
        hidden0,
        q0,
        k0,
        v0,
        w_first,
        cosine,
        sine,
    )
    along = along[:, 0]
    top_hidden = jnp.concatenate(
        [hidden0[i * seq_len : i * seq_len + slots] for i in range(micro)], axis=0
    ).astype(f32)
    top_grad = jnp.concatenate(
        [grad[i * seq_len : i * seq_len + slots] for i in range(micro)], axis=0
    )
    along_high = along.astype(bf16)
    along_low = (along - along_high.astype(f32)).astype(bf16)
    extra = jnp.zeros((8, cols), bf16)
    extra = extra.at[0, :cells].set(along_high).at[1, :cells].set(along_low)
    chunks = jnp.concatenate(
        [
            jnp.transpose(partial.reshape(cells, line, cols), (1, 0, 2)),
            jnp.broadcast_to(extra[None], (line,) + extra.shape),
        ],
        axis=1,
    )
    summed = jnp.sum(exchange(chunks, LINE).astype(f32), axis=0)
    d_normed = summed[:cells]
    along = (summed[cells, :cells] + summed[cells + 1, :cells])[:, None]
    factor = inverse_rms(top_hidden)
    hidden_cols = lax.dynamic_slice_in_dim(top_hidden, place * cols, cols, 1)
    grad_cols = lax.dynamic_slice_in_dim(top_grad, place * cols, cols, 1).astype(f32)
    new_grad = (grad_cols + factor * d_normed - hidden_cols * factor**3 * along).astype(bf16)
    d_image = jnp.concatenate(
        [
            dot_tn(placing[i], new_grad[i * slots : (i + 1) * slots]).astype(bf16)
            for i in range(micro)
        ],
        axis=0,
    )
    proj_part = dot_tn(encoded, d_image).astype(bf16)
    owners = 2 * dp_size
    parts = exchange(proj_part.reshape(owners, depth // owners, cols), ("segment", "dp"))
    parts = jnp.sum(parts.astype(f32).reshape(2, dp_size, depth // owners, cols), axis=1)
    projector_grad = jnp.transpose(parts, (1, 0, 2)).reshape(depth // owners, 2 * cols)
    return (loss, projector_grad)


def solution(mesh):
    placed = (
        P(None, "dp", None, None),
        P(None, "dp", None, None),
        P(),
        P(None, "dp"),
        P(None, "dp", None),
        P(None, "dp", None),
        P(),
        P(None, None, "vocab"),
        P(None, "vocab", None),
        P(None, "vocab"),
        P("segment", None, "dp", "vocab"),
        P("segment", "vocab", "dp"),
        P(("segment", "dp", "vocab"), None),
        P(None, ("segment", "dp", "vocab")),
    )
    return jax.shard_map(
        shards,
        mesh=mesh,
        in_specs=placed,
        out_specs=(P(), P(("segment", "dp"), "vocab")),
        check_vma=False,
    )
```

time: 432 us -> 954 us (2.21)
  Pallas kernels: 0 us -> 577 us
  blocking collectives: 56.7 us -> 0 us
  waiting for transfers between devices: 152 us -> 208 us
  matrix products: 58.6 us -> 4.83 us
  starting transfers between devices: 55.4 us -> 87.1 us
  local copies, waits for them, and re-layouts: 56.5 us -> 42.2 us
  between operations: 17.2 us -> 3.56 us
  other arithmetic: 33.8 us -> 21.8 us
    pallas_call x0 -> x10, Pallas kernels: none -> 577 us  [the longest x2 512 us: collected(): pl.pallas_call(collect, name='collect', out_shape=jax.ShapeDtypeStruct((1...]
    ppermute x0 -> x24, waiting for transfers between devices: none -> 100 us  [the longest x12 74.5 us: side_shift(): return lax.ppermute(block, SIDE, route)]
    all_to_all x2 -> x0, blocking collectives: 46.5 us -> none  [exchange(): return lax.all_to_all(chunks, axes, 0, 0, tiled=True)]
    all_gather x2 -> x0, waiting for transfers between devices: 33.1 us -> none  [shards(): lax.all_gather(jnp.transpose(part, (1, 0, 2)).reshape(rows_here, 4 * half...]
    ppermute x0 -> x24, starting transfers between devices: none -> 32.9 us  [the longest x12 18 us: side_shift(): return lax.ppermute(block, SIDE, route)]
    dot_general x11 -> x1, matrix products: 32.5 us -> 0.51 us  [dot(): return jnp.dot(a, b, preferred_element_type=f32)]
    slice x8 -> x7, local copies, waits for them, and re-layouts: 29.7 us -> 10.4 us  [the longest x2 3.61 us: gather_weights(): high = side_shift(from_ahead[2:], -1, False)]
    all_to_all x9 -> x8, waiting for transfers between devices: 98.1 us -> 78.8 us  [exchange(): return lax.all_to_all(chunks, axes, 0, 0, tiled=True)]
  transfers between devices with their start and end apart: 18 -> 44, of which waited for: 12 -> 29; matrix products, arithmetic and copies ran while one was open for 20% -> 3% of each run, Pallas kernels for 0% -> 58%
where the time goes in v2:
time: 954 us; the launch traced here: 944 us
  Pallas kernels  577 us (60%)
  waiting for transfers between devices  208 us (22%)
  starting transfers between devices  87.1 us (9%)
  local copies, waits for them, and re-layouts  42.2 us (4%)
  other arithmetic  21.8 us (2%)
    pallas_call x2, Pallas kernels, collected(): pl.pallas_call(collect, name='collect', out_shape=jax.ShapeDtypeStruct((1...  512 us
    all_to_all x8, waiting for transfers between devices, exchange(): return lax.all_to_all(chunks, axes, 0, 0, tiled=True)  78.8 us
    ppermute x12, waiting for transfers between devices, side_shift(): return lax.ppermute(block, SIDE, route)  74.5 us
    pallas_call x8, Pallas kernels, call(): pl.pallas_call(body, name=name, out_shape=[jax.ShapeDtypeStruct(shape, ki...  64.8 us
    all_to_all x8, starting transfers between devices, exchange(): return lax.all_to_all(chunks, axes, 0, 0, tiled=True)  44.9 us
    ppermute x12, waiting for transfers between devices, swap(): lax.ppermute(block, axis, [(i, i ^ mask) for i in range(lax.axis_size(axi...  28.8 us
    ppermute x12, waiting for transfers between devices, line_move(): return lax.ppermute(block, TOKENS, route)  25.6 us
  transfers between devices with their start and end apart: 44, of which 29 were waited for; matrix products, arithmetic and copies ran while one was open for 3% of the time, Pallas kernels for 58%

profile of v2, /device:TPU:2, one launch (start us, length us, event | category | flops | bytes accessed | tf_op | source)
XLA Modules:
  0.0 944.0 jit_solution(14507384926777264819)
XLA Ops:
  3.7 13.2 %collective-permute-done.6 = bf16[4,256,256]{2,1,0:T(8,128)(2,1)S(1)} collective-permute-done((bf16[4,256,256]{2,1,0:T(8,128)(2,1)S(1)}, bf16[4,256,256]{2,1,0:T(8,128)(2,1)S(1)}, u32[]{:S(2)}, u32[]{:S(2)}) %collective-permute-start.6) | collective-permute-done | bytes 524320 | tf_op jit(solution)/shard_map/ppermute | solution.py:36
  19.6 2.3 copy.76
  24.1 1.6 collective-permute-start.8
  25.7 1.7 collective-permute-start.7
  27.4 13.0 %collective-permute-done.8 = bf16[2,256,1024]{2,1,0:T(8,128)(2,1)S(1)} collective-permute-done((bf16[2,256,1024]{2,1,0:T(8,128)(2,1)}, bf16[2,256,1024]{2,1,0:T(8,128)(2,1)S(1)}, u32[]{:S(2)}, u32[]{:S(2)}) %collective-permute-start.8) | collective-permute-done | bytes 1048608 | tf_op jit(solution)/shard_map/ppermute | solution.py:102
  42.8 8.9 collective-permute-done.9
  51.7 1.6 pad_maximum_fusion.near
  53.3 1.9 collective-permute-start.11
  55.2 2.1 collective-permute-start.10
  57.3 24.3 %collective-permute-done.11.behind = bf16[4,256,1024]{2,1,0:T(8,128)(2,1)} collective-permute-done((bf16[4,256,1024]{2,1,0:T(8,128)(2,1)}, bf16[4,256,1024]{2,1,0:T(8,128)(2,1)}, u32[]{:S(2)}, u32[]{:S(2)}) %collective-permute-start.11) | collective-permute-done | bytes 2097184 | tf_op jit(solution)/shard_map/ppermute | solution.py:102
  81.7 2.3 slice.142
  83.9 2.3 slice.143
  86.3 3.2 collective-permute-start.13
  90.9 9.1 prepare.1
  100.1 7.0 encode_first.1.p0
  107.1 2.1 collective-permute-start.1
  110.5 3.4 collective-permute-done.1.p2
  113.9 1.7 collective-permute-done.2.p3
  116.2 7.2 encode_next.1
  123.7 2.1 collective-permute-start.4
  127.0 3.4 collective-permute-done.4.p2
  130.4 1.9 collective-permute-done.5.p3
  132.9 3.1 encode_last.1
  136.0 1.8 broadcast_in_dim.44
  137.9 4.9 all-to-all-start
  145.6 256.0 %collect.2.w = bf16[4096,1024]{1,0:T(8,128)(2,1)} custom-call(s32[16]{0:T(128)} %select_n.157.targets, bf16[4,256,1024]{2,1,0:T(8,128)(2,1)} %pad_maximum_fusion.near, bf16[4,256,1024]{2,1,0:T(8,128)(2,1)} %collective-permute-done.10.ahead, bf16[2,256,1024]{2,1,0:T(8,128)(2,1)} %collective-permute-done.12.far_low, ...), custom_call_target="tpu_custom_call" | custom-call | tf_op jit(solution)/shard_map/collect/pallas_call | solution.py:360
  402.5 9.8 %first_section.1 = (bf16[192,4096]{1,0:T(8,128)(2,1)}, bf16[192,256]{1,0:T(8,128)(2,1)}, bf16[192,256]{1,0:T(8,128)(2,1)}, bf16[192,256]{1,0:T(8,128)(2,1)}, bf1...) custom-call(bf16[8,36,1024]{2,1,0:T(8,128)(2,1)} %copy-done.6, bf16[2,96,4096]{2,1,0:T(8,128)(2,1)} %bitcast.169, ...), custom_call_target="tpu_custom_call" | custom-call | tf_op jit(solution)/shard_map/first_section/pallas_call | solution.py:80
  413.8 2.6 pad_maximum_fusion.1.near
  417.6 2.0 collective-permute-start.23
  422.4 2.6 collective-permute-start.16
  425.6 18.4 %collective-permute-done.24.behind = bf16[4,256,1024]{2,1,0:T(8,128)(2,1)} collective-permute-done((bf16[4,256,1024]{2,1,0:T(8,128)(2,1)}, bf16[4,256,1024]{2,1,0:T(8,128)(2,1)}, u32[]{:S(2)}, u32[]{:S(2)}) %collective-permute-start.24) | collective-permute-done | bytes 2097184 | tf_op jit(solution)/shard_map/ppermute | solution.py:102
  446.7 3.3 collective-permute-start.26
  452.4 9.0 collective-permute-done.25.far_low
  462.3 256.0 %collect.3.w = bf16[4096,1024]{1,0:T(8,128)(2,1)} custom-call(s32[16]{0:T(128)} %select_n.157.targets, bf16[4,256,1024]{2,1,0:T(8,128)(2,1)} %pad_maximum_fusion.1.near, bf16[4,256,1024]{2,1,0:T(8,128)(2,1)} %collective-permute-done.23.ahead, bf16[2,256,1024]{2,1,0:T(8,128)(2,1)} %collective-permute-done.25.far_low, ...), custom_call_target="tpu_custom_call" | custom-call | tf_op jit(solution)/shard_map/collect/pallas_call | solution.py:360
  718.3 2.2 collective-permute-start.19
  720.5 5.1 collective-permute-done.19
  725.6 3.7 collective-permute-done.20
  729.9 2.0 collective-permute-done.21
  733.2 9.0 last_section.1
  742.2 4.5 all-to-all-start.1
  746.7 4.2 all-to-all-done.1
  752.6 7.0 all-to-all-start.2
  760.4 17.0 %all-to-all-done.2 = bf16[128,8,512]{2,1,0:T(8,128)(2,1)S(1)} async-done(((bf16[128,8,512]{2,1,0:T(8,128)(2,1)}), bf16[128,8,512]{2,1,0:T(8,128)(2,1)S(1)}, u32[]{:S(2)}, u32[]{:S(2)}) %all-to-all-start.2) | async-done | bytes 1048608 | tf_op jit(solution)/shard_map/all_to_all | solution.py:40
  779.0 2.2 exponential_reduce_fusion.1
  781.9 5.5 all-to-all-start.3
  787.7 9.9 %all-to-all-done.3 = f32[128,4,128]{2,1,0:T(4,128)S(1)} async-done(((f32[128,4,128]{2,1,0:T(4,128)}), f32[128,4,128]{2,1,0:T(4,128)S(1)}, u32[]{:S(2)}, u32[]{:S(2)}) %all-to-all-start.3) | async-done | bytes 262176 | tf_op jit(solution)/shard_map/all_to_all | solution.py:40
  800.2 5.0 all-to-all-start.4
  806.5 16.7 %all-to-all-done.4 = bf16[128,8,512]{2,1,0:T(8,128)(2,1)S(1)} async-done(((bf16[128,8,512]{2,1,0:T(8,128)(2,1)}), bf16[128,8,512]{2,1,0:T(8,128)(2,1)S(1)}, u32[]{:S(2)}, u32[]{:S(2)}) %all-to-all-start.4) | async-done | bytes 1048608 | tf_op jit(solution)/shard_map/all_to_all | solution.py:40
  824.0 5.3 all-to-all-start.5
  830.0 3.5 all-to-all-done.5
  836.1 9.5 %last_section_back.1 = (bf16[192,4096]{1,0:T(8,128)(2,1)}, bf16[192,768]{1,0:T(8,128)(2,1)}) custom-call(bf16[8,4096]{1,0:T(8,128)(2,1)} %fusion.24.grad, bf16[8,192]{1,0:T(8,128)(2,1)} %get-tuple-element.57.pick, bf16[8,256]{1,0:T(8,128)(2,1)} %get-tuple-element.61.q, bf16[192,256]{1,0:T(8,128)(2,1)} %get-tuple-element.62.k, ...), custom_call_target="tpu_custom_call" | custom-call | tf_op jit(solution)/shard_map/last_section_back/pallas_call | solution.py:80
  851.4 2.0 collective-permute-start.31
  854.8 2.6 collective-permute-done.29
  857.4 3.3 collective-permute-done.30
  860.7 1.7 collective-permute-done.31
  865.0 3.5 collective-permute-start.32
  870.1 3.8 collective-permute-done.32
  873.9 4.0 collective-permute-done.33
  879.7 2.0 collective-permute-done.35
  883.0 10.0 %first_section_back.1 = (bf16[72,4096]{1,0:T(8,128)(2,1)}, f32[72,1]{1,0:T(8,128)}, f32[72,768]{1,0:T(8,128)}) custom-call(bf16[192,4096]{1,0:T(8,128)(2,1)} %bitcast.152, bf16[192,4096]{1,0:T(8,128)(2,1)} %get-tuple-element.55.hidden, bf16[192,256]{1,0:T(8,128)(2,1)} %get-tuple-element.65.q, bf16[192,256]{1,0:T(8,128)(2,1)} %get-tuple-element.66.k, ...), custom_call_target="tpu_custom_call" | custom-call | tf_op jit(solution)/shard_map/first_section_back/pallas_call | solution.py:80
  896.1 6.7 all-to-all-start.6
  904.0 9.2 all-to-all-done.6
  916.4 5.9 all-to-all-start.7
  923.0 18.3 %all-to-all-done.7 = bf16[32,36,512]{2,1,0:T(8,128)(2,1)S(1)} async-done(((bf16[32,36,512]{2,1,0:T(8,128)(2,1)}), bf16[32,36,512]{2,1,0:T(8,128)(2,1)S(1)}, u32[]{:S(2)}, u32[]{:S(2)}) %all-to-all-start.7) | async-done | bytes 1179680 | tf_op jit(solution)/shard_map/all_to_all | solution.py:40
  (202 shorter events, 69.2 us)
Async XLA Ops:
  0.6 778.3 %copy-start = (bf16[256,4096]{1,0:T(8,128)(2,1)S(1)}, bf16[256,4096]{1,0:T(8,128)(2,1)}, u32[]{:S(2)}) copy-start(bf16[256,4096]{1,0:T(8,128)(2,1)} %param.30) | copy-start | bytes 6291460
  0.6 16.3 %copy-start.5 = (bf16[1,3,256,512]{3,2,1,0:T(8,128)(2,1)S(1)}, bf16[1,3,256,512]{3,2,1,0:T(8,128)(2,1)}, u32[]{:S(2)}) copy-start(bf16[1,3,256,512]{3,2,1,0:T(8,128)(2,1)} %param.28) | copy-start | bytes 2359300
  3.2 13.7 %collective-permute-start.6 = (bf16[4,256,256]{2,1,0:T(8,128)(2,1)S(1)}, bf16[4,256,256]{2,1,0:T(8,128)(2,1)S(1)}, u32[]{:S(2)}, u32[]{:S(2)}) collective-permute-start(bf16[4,256,256]{2,1,0:T(8,128)(2,1)S(1)} %broadcast_select_fusion), channel_id=1, source_target_pairs={{0,64},{64,0},{1,65},{65,1},{2,66},{66,2},{3,67},{67,3},{4,68},{68... | collective-permute-start | bytes 1572872 | tf_op jit(solution)/shard_map/ppermute | solution.py:36
  24.1 16.2 %collective-permute-start.8 = (bf16[2,256,1024]{2,1,0:T(8,128)(2,1)}, bf16[2,256,1024]{2,1,0:T(8,128)(2,1)S(1)}, u32[]{:S(2)}, u32[]{:S(2)}) collective-permute-start(bf16[2,256,1024]{2,1,0:T(8,128)(2,1)} %constant_dynamic-update-slice_fusion), channel_id=1, source_target_pairs={{0,4},{1,17},{2,6},{3,19},{4,8},{5,21},{6,10},{7,23},{8,12},{9,25}... | collective-permute-start | bytes 3145736 | tf_op jit(solution)/shard_map/ppermute | solution.py:102
  25.7 16.0 %collective-permute-start.7 = (bf16[2,256,1024]{2,1,0:T(8,128)(2,1)}, bf16[2,256,1024]{2,1,0:T(8,128)(2,1)S(1)}, u32[]{:S(2)}, u32[]{:S(2)}) collective-permute-start(bf16[2,256,1024]{2,1,0:T(8,128)(2,1)} %constant_dynamic-update-slice_fusion), channel_id=1, source_target_pairs={{0,12},{1,49},{2,14},{3,51},{4,0},{5,53},{6,2},{7,55},{8,4},{9,57}... | collective-permute-start | bytes 3145736 | tf_op jit(solution)/shard_map/ppermute | solution.py:102
  41.3 10.4 %collective-permute-start.9 = (bf16[256,1024]{1,0:T(8,128)(2,1)S(1)}, bf16[256,1024]{1,0:T(8,128)(2,1)S(1)}, u32[]{:S(2)}, u32[]{:S(2)}) collective-permute-start(bf16[256,1024]{1,0:T(8,128)(2,1)S(1)} %get-tuple-element.92), channel_id=1, source_target_pairs={{0,4},{1,17},{2,6},{3,19},{4,8},{5,21},{6,10},{7,23},{8,12},{9,25}... | collective-permute-start | bytes 1572872 | tf_op jit(solution)/shard_map/ppermute | solution.py:102
  53.3 28.4 %collective-permute-start.11 = (bf16[4,256,1024]{2,1,0:T(8,128)(2,1)}, bf16[4,256,1024]{2,1,0:T(8,128)(2,1)}, u32[]{:S(2)}, u32[]{:S(2)}) collective-permute-start(bf16[4,256,1024]{2,1,0:T(8,128)(2,1)} %pad_maximum_fusion.near), channel_id=1, source_target_pairs={{0,16},{1,5},{2,18},{3,7},{4,20},{5,9},{6,22},{7,11},{8,24},{9,13}... | collective-permute-start | bytes 6291464 | tf_op jit(solution)/shard_map/ppermute | solution.py:102
  55.2 28.7 %collective-permute-start.10 = (bf16[4,256,1024]{2,1,0:T(8,128)(2,1)}, bf16[4,256,1024]{2,1,0:T(8,128)(2,1)}, u32[]{:S(2)}, u32[]{:S(2)}) collective-permute-start(bf16[4,256,1024]{2,1,0:T(8,128)(2,1)} %pad_maximum_fusion.near), channel_id=1, source_target_pairs={{0,48},{1,13},{2,50},{3,15},{4,52},{5,1},{6,54},{7,3},{8,56},{9,5}... | collective-permute-start | bytes 6291464 | tf_op jit(solution)/shard_map/ppermute | solution.py:102
  83.9 5.5 copy-start.12
  83.9 6.4 copy-start.25
  83.9 61.7 %collective-permute-start.12 = (bf16[2,256,1024]{2,1,0:T(8,128)(2,1)}, bf16[2,256,1024]{2,1,0:T(8,128)(2,1)}, u32[]{:S(2)}, u32[]{:S(2)}) collective-permute-start(bf16[2,256,1024]{2,1,0:T(8,128)(2,1)} %slice.142), channel_id=1, source_target_pairs={{0,16},{1,5},{2,18},{3,7},{4,20},{5,9},{6,22},{7,11},{8,24},{9,13}... | collective-permute-start | bytes 3145736 | tf_op jit(solution)/shard_map/ppermute | solution.py:102
  86.3 59.3 %collective-permute-start.13 = (bf16[2,256,1024]{2,1,0:T(8,128)(2,1)}, bf16[2,256,1024]{2,1,0:T(8,128)(2,1)}, u32[]{:S(2)}, u32[]{:S(2)}) collective-permute-start(bf16[2,256,1024]{2,1,0:T(8,128)(2,1)} %slice.143), channel_id=1, source_target_pairs={{0,48},{1,13},{2,50},{3,15},{4,52},{5,1},{6,54},{7,3},{8,56},{9,5}... | collective-permute-start | bytes 3145736 | tf_op jit(solution)/shard_map/ppermute | solution.py:102
  107.1 3.4 collective-permute-start
  107.1 6.8 collective-permute-start.1
  109.3 6.4 collective-permute-start.2
  110.5 5.1 copy-start.13
  113.9 1.7 copy-start.14
  123.5 3.5 collective-permute-start.3
  123.7 6.7 collective-permute-start.4
  125.8 6.5 collective-permute-start.5
  127.0 5.3 copy-start.16
  130.4 1.9 copy-start.17
  136.0 7.4 copy-start.23
  137.9 263.8 %all-to-all-start = ((bf16[8,36,1024]{2,1,0:T(8,128)(2,1)}), bf16[8,36,1024]{2,1,0:T(8,128)(2,1)S(1)}, u32[]{:S(2)}, u32[]{:S(2)}) async-start(bf16[8,36,1024]{2,1,0:T(8,128)(2,1)} %broadcast_in_dim.44), calls=%async_computation | async-start | bytes 1310720 | tf_op jit(solution)/shard_map/all_to_all | solution.py:40
  145.0 268.8 %collective-permute-start.22 = (bf16[256,1024]{1,0:T(8,128)(2,1)}, bf16[256,1024]{1,0:T(8,128)(2,1)}, u32[]{:S(2)}, u32[]{:S(2)}) collective-permute-start(bf16[256,1024]{1,0:T(8,128)(2,1)} %get-tuple-element.89), channel_id=1, source_target_pairs={{0,12},{1,49},{2,14},{3,51},{4,0},{5,53},{6,2},{7,55},{8,4},{9,57}... | collective-permute-start | bytes 1572872 | tf_op jit(solution)/shard_map/ppermute | solution.py:102
  412.3 1.5 copy-start.7
  412.3 1.5 copy-start.8
  413.6 6.1 collective-permute-start.14
  416.4 27.6 %collective-permute-start.24 = (bf16[4,256,1024]{2,1,0:T(8,128)(2,1)}, bf16[4,256,1024]{2,1,0:T(8,128)(2,1)}, u32[]{:S(2)}, u32[]{:S(2)}) collective-permute-start(bf16[4,256,1024]{2,1,0:T(8,128)(2,1)} %pad_maximum_fusion.1.near), channel_id=1, source_target_pairs={{0,16},{1,5},{2,18},{3,7},{4,20},{5,9},{6,22},{7,11},{8,24},{9,13}... | collective-permute-start | bytes 6291464 | tf_op jit(solution)/shard_map/ppermute | solution.py:102
  417.6 27.7 %collective-permute-start.23 = (bf16[4,256,1024]{2,1,0:T(8,128)(2,1)}, bf16[4,256,1024]{2,1,0:T(8,128)(2,1)}, u32[]{:S(2)}, u32[]{:S(2)}) collective-permute-start(bf16[4,256,1024]{2,1,0:T(8,128)(2,1)} %pad_maximum_fusion.1.near), channel_id=1, source_target_pairs={{0,48},{1,13},{2,50},{3,15},{4,52},{5,1},{6,54},{7,3},{8,56},{9,5}... | collective-permute-start | bytes 6291464 | tf_op jit(solution)/shard_map/ppermute | solution.py:102
  422.1 27.9 %collective-permute-start.15 = (bf16[24,4096]{1,0:T(8,128)(2,1)}, bf16[24,4096]{1,0:T(8,128)(2,1)S(1)}, u32[]{:S(2)}, u32[]{:S(2)}) collective-permute-start(bf16[24,4096]{1,0:T(8,128)(2,1)} %get-tuple-element.97), channel_id=1, source_target_pairs={{0,64},{1,65},{2,66},{3,67},{64,0},{65,1},{66,2},{67,3},{4,68},{5,... | collective-permute-start | bytes 589832 | tf_op jit(solution)/shard_map/ppermute | solution.py:112
  422.4 27.6 %collective-permute-start.16 = (bf16[24,4096]{1,0:T(8,128)(2,1)}, bf16[24,4096]{1,0:T(8,128)(2,1)S(1)}, u32[]{:S(2)}, u32[]{:S(2)}) collective-permute-start(bf16[24,4096]{1,0:T(8,128)(2,1)} %get-tuple-element.99), channel_id=1, source_target_pairs={{0,2},{1,3},{2,0},{3,1},{64,66},{65,67},{66,64},{67,65},{4,6},{5,7... | collective-permute-start | bytes 589832 | tf_op jit(solution)/shard_map/ppermute | solution.py:112
  425.0 25.0 %collective-permute-start.17 = (bf16[24,4096]{1,0:T(8,128)(2,1)S(1)}, bf16[24,4096]{1,0:T(8,128)(2,1)}, u32[]{:S(2)}, u32[]{:S(2)}) collective-permute-start(bf16[24,4096]{1,0:T(8,128)(2,1)S(1)} %get-tuple-element.98), channel_id=1, source_target_pairs={{0,66},{1,67},{2,64},{3,65},{64,2},{65,3},{66,0},{67,1},{4,70},{5,... | collective-permute-start | bytes 589832 | tf_op jit(solution)/shard_map/ppermute | solution.py:112
  445.3 16.2 %collective-permute-start.25 = (bf16[2,256,1024]{2,1,0:T(8,128)(2,1)S(1)}, bf16[2,256,1024]{2,1,0:T(8,128)(2,1)}, u32[]{:S(2)}, u32[]{:S(2)}) collective-permute-start(bf16[2,256,1024]{2,1,0:T(8,128)(2,1)S(1)} %slice.146), channel_id=1, source_target_pairs={{0,16},{1,5},{2,18},{3,7},{4,20},{5,9},{6,22},{7,11},{8,24},{9,13}... | collective-permute-start | bytes 3145736 | tf_op jit(solution)/shard_map/ppermute | solution.py:102
  446.7 15.6 %collective-permute-start.26 = (bf16[2,256,1024]{2,1,0:T(8,128)(2,1)S(1)}, bf16[2,256,1024]{2,1,0:T(8,128)(2,1)}, u32[]{:S(2)}, u32[]{:S(2)}) collective-permute-start(bf16[2,256,1024]{2,1,0:T(8,128)(2,1)S(1)} %slice.147), channel_id=1, source_target_pairs={{0,48},{1,13},{2,50},{3,15},{4,52},{5,1},{6,54},{7,3},{8,56},{9,5}... | collective-permute-start | bytes 3145736 | tf_op jit(solution)/shard_map/ppermute | solution.py:102
  452.1 268.4 %copy-start.4 = (bf16[4,24,4096]{2,1,0:T(8,128)(2,1)S(1)}, bf16[4,24,4096]{2,1,0:T(8,128)(2,1)}, u32[]{:S(2)}) copy-start(bf16[4,24,4096]{2,1,0:T(8,128)(2,1)} %copy-done.3) | copy-start | bytes 2359300
  452.1 268.4 %collective-permute-start.18 = (bf16[24,4096]{1,0:T(8,128)(2,1)S(1)}, bf16[24,4096]{1,0:T(8,128)(2,1)S(1)}, u32[]{:S(2)}, u32[]{:S(2)}) collective-permute-start(bf16[24,4096]{1,0:T(8,128)(2,1)S(1)} %get-tuple-element.81), channel_id=1, source_target_pairs={{0,64},{1,65},{2,66},{3,67},{64,0},{65,1},{66,2},{67,3},{4,68},{5,... | collective-permute-start | bytes 589832 | tf_op jit(solution)/shard_map/ppermute | solution.py:112
  718.3 7.3 collective-permute-start.19
  720.5 8.9 collective-permute-start.20
  729.4 2.6 collective-permute-start.21
  742.2 8.7 all-to-all-start.1
  751.6 8.0 copy-start.20
  752.6 24.8 %all-to-all-start.2 = ((bf16[128,8,512]{2,1,0:T(8,128)(2,1)}), bf16[128,8,512]{2,1,0:T(8,128)(2,1)S(1)}, u32[]{:S(2)}, u32[]{:S(2)}) async-start(bf16[128,8,512]{2,1,0:T(8,128)(2,1)} %broadcast_in_dim.105), calls=%async_computation.2 | async-start | bytes 2097152 | tf_op jit(solution)/shard_map/all_to_all | solution.py:40
  779.0 8.5 copy-start.24
  781.9 15.7 %all-to-all-start.3 = ((f32[128,4,128]{2,1,0:T(4,128)}), f32[128,4,128]{2,1,0:T(4,128)S(1)}, u32[]{:S(2)}, u32[]{:S(2)}) async-start(f32[128,4,128]{2,1,0:T(4,128)} %broadcast_in_dim.106), calls=%async_computation.3 | async-start | bytes 524288 | tf_op jit(solution)/shard_map/all_to_all | solution.py:40
  800.2 5.0 copy-start.19
  800.2 23.0 %all-to-all-start.4 = ((bf16[128,8,512]{2,1,0:T(8,128)(2,1)}), bf16[128,8,512]{2,1,0:T(8,128)(2,1)S(1)}, u32[]{:S(2)}, u32[]{:S(2)}) async-start(bf16[128,8,512]{2,1,0:T(8,128)(2,1)} %bitcast.159), calls=%async_computation.4 | async-start | bytes 2097152 | tf_op jit(solution)/shard_map/all_to_all | solution.py:40
  805.2 24.1 %collective-permute-start.27 = (bf16[36,1152]{1,0:T(8,128)(2,1)S(1)}, bf16[36,1152]{1,0:T(8,128)(2,1)S(1)}, u32[]{:S(2)}, u32[]{:S(2)}) collective-permute-start(bf16[36,1152]{1,0:T(8,128)(2,1)S(1)} %copy-done.19), channel_id=1, source_target_pairs={{0,64},{64,0},{1,65},{65,1},{2,66},{66,2},{3,67},{67,3},{4,68},{68... | collective-permute-start | bytes 248840 | tf_op jit(solution)/shard_map/ppermute | solution.py:36
  824.0 9.5 %all-to-all-start.5 = ((bf16[8,8,512]{2,1,0:T(8,128)(2,1)}), bf16[8,8,512]{2,1,0:T(8,128)(2,1)S(1)}, u32[]{:S(2)}, u32[]{:S(2)}) async-start(bf16[8,8,512]{2,1,0:T(8,128)(2,1)} %broadcast_in_dim.107), calls=%async_computation.5 | async-start | bytes 131072 | tf_op jit(solution)/shard_map/all_to_all | solution.py:40
  845.6 3.7 copy-start.9
  847.0 2.4 collective-permute-start.28
  849.6 7.8 collective-permute-start.29
  851.1 9.5 %collective-permute-start.30 = (bf16[24,4096]{1,0:T(8,128)(2,1)S(1)}, bf16[24,4096]{1,0:T(8,128)(2,1)S(1)}, u32[]{:S(2)}, u32[]{:S(2)}) collective-permute-start(bf16[24,4096]{1,0:T(8,128)(2,1)S(1)} %get-tuple-element.96), channel_id=1, source_target_pairs={{0,2},{1,3},{2,0},{3,1},{64,66},{65,67},{66,64},{67,65},{4,6},{5,7... | collective-permute-start | bytes 589832 | tf_op jit(solution)/shard_map/ppermute | solution.py:112
  851.4 10.9 %collective-permute-start.31 = (bf16[24,4096]{1,0:T(8,128)(2,1)S(1)}, bf16[24,4096]{1,0:T(8,128)(2,1)S(1)}, u32[]{:S(2)}, u32[]{:S(2)}) collective-permute-start(bf16[24,4096]{1,0:T(8,128)(2,1)S(1)} %get-tuple-element.95), channel_id=1, source_target_pairs={{0,66},{1,67},{2,64},{3,65},{64,2},{65,3},{66,0},{67,1},{4,70},{5,... | collective-permute-start | bytes 589832 | tf_op jit(solution)/shard_map/ppermute | solution.py:112
  854.5 9.1 copy-start.10
  854.5 9.1 copy-start.22
  865.0 8.9 collective-permute-start.32
  868.5 9.4 collective-permute-start.33
  869.5 9.8 %collective-permute-start.34 = (bf16[24,4096]{1,0:T(8,128)(2,1)S(1)}, bf16[24,4096]{1,0:T(8,128)(2,1)S(1)}, u32[]{:S(2)}, u32[]{:S(2)}) collective-permute-start(bf16[24,4096]{1,0:T(8,128)(2,1)S(1)} %get-tuple-element.119), channel_id=1, source_target_pairs={{0,66},{1,67},{2,64},{3,65},{64,2},{65,3},{66,0},{67,1},{4,70},{5,... | collective-permute-start | bytes 589832 | tf_op jit(solution)/shard_map/ppermute | solution.py:112
  879.4 2.4 collective-permute-start.35
  896.1 17.0 %all-to-all-start.6 = ((bf16[8,80,512]{2,1,0:T(8,128)(2,1)}), bf16[8,80,512]{2,1,0:T(8,128)(2,1)S(1)}, u32[]{:S(2)}, u32[]{:S(2)}) async-start(bf16[8,80,512]{2,1,0:T(8,128)(2,1)} %pad_maximum_fusion.2), calls=%async_computation.6 | async-start | bytes 1310720 | tf_op jit(solution)/shard_map/all_to_all | solution.py:40
  902.8 11.5 %copy-start.21 = (bf16[2,36,36]{2,1,0:T(8,128)(2,1)S(1)}, bf16[2,36,36]{2,1,0:T(8,128)(2,1)}, u32[]{:S(2)}) copy-start(bf16[2,36,36]{2,1,0:T(8,128)(2,1)} %get-tuple-element.53.placing) | copy-start | bytes 15556
  913.2 1.5 copy-start.11
  916.4 24.9 %all-to-all-start.7 = ((bf16[32,36,512]{2,1,0:T(8,128)(2,1)}), bf16[32,36,512]{2,1,0:T(8,128)(2,1)S(1)}, u32[]{:S(2)}, u32[]{:S(2)}) async-start(bf16[32,36,512]{2,1,0:T(8,128)(2,1)} %reshape.352), calls=%async_computation.7 | async-start | bytes 2621440 | tf_op jit(solution)/shard_map/all_to_all | solution.py:40
  (6 other events, 5.3 us)
